TPU v7x, 32 devices: a whole 2x2x4 slice. The times are simulated.
32 devices in a mesh: dp: 8 (over z, x), height: 4 (over y, core).
Axes of the slice: x: 2, y: 2, z: 4, core: 2. Of those that a mesh axis runs over, the one named last changes fastest.
Arguments:
- images: bfloat16 [48, 32, 32, 512], P('dp', 'height'), may hold values from -6 to 6
- size_group: int32 [48], P('dp'), may hold values from 0 to 2
- cotangent: bfloat16 [48, 16, 16, 1024], P('dp', 'height'), may hold values from -6 to 6
- reduce_one: bfloat16 [131072], P(('dp', 'height')), may hold values from -0.25 to 0.25
- split_one: bfloat16 [589824], P(('dp', 'height')), may hold values from -0.1875 to 0.1875
- squeeze_one: bfloat16 [32768], P(('dp', 'height')), may hold values from -0.375 to 0.375
- expand_one: bfloat16 [65536], P(('dp', 'height')), may hold values from -0.5 to 0.5
- output_one: bfloat16 [262144], P(('dp', 'height')), may hold values from -0.375 to 0.375
- shortcut: bfloat16 [524288], P(('dp', 'height')), may hold values from -0.25 to 0.25
- reduce_two: bfloat16 [262144], P(('dp', 'height')), may hold values from -0.1875 to 0.1875
- split_two: bfloat16 [589824], P(('dp', 'height')), may hold values from -0.1875 to 0.1875
- squeeze_two: bfloat16 [32768], P(('dp', 'height')), may hold values from -0.375 to 0.375
- expand_two: bfloat16 [65536], P(('dp', 'height')), may hold values from -0.5 to 0.5
- output_two: bfloat16 [262144], P(('dp', 'height')), may hold values from -0.375 to 0.375
- norm_gains: bfloat16 [4864], P(('dp', 'height')), may hold values from 0.099609375 to 1.8984375
- norm_shifts: bfloat16 [5888], P(('dp', 'height')), may hold values from -3 to 3
Outputs:
- layer_one: bfloat16 [48, 16, 16, 1024], P('dp', 'height')
- layer_two: bfloat16 [48, 16, 16, 1024], P('dp', 'height')
- grad_images: bfloat16 [48, 32, 32, 512], P('dp', 'height')
- grad_reduce_one: float32 [131072], P(('dp', 'height'))
- grad_split_one: float32 [589824], P(('dp', 'height'))
- grad_squeeze_one: float32 [32768], P(('dp', 'height'))
- grad_expand_one: float32 [65536], P(('dp', 'height'))
- grad_output_one: float32 [262144], P(('dp', 'height'))
- grad_shortcut: float32 [524288], P(('dp', 'height'))
- grad_reduce_two: float32 [262144], P(('dp', 'height'))
- grad_split_two: float32 [589824], P(('dp', 'height'))
- grad_squeeze_two: float32 [32768], P(('dp', 'height'))
- grad_expand_two: float32 [65536], P(('dp', 'height'))
- grad_output_two: float32 [262144], P(('dp', 'height'))
- grad_gains: float32 [4864], P(('dp', 'height'))
- grad_shifts: float32 [5888], P(('dp', 'height'))
Inputs may be any that keep to these rules, and one draw needn't show every extreme that they name: `size_group`: size group of each image: its valid grid is 32 - 4 * (2 - group) cells on a side, in the top-left corner; the other cells are ignored.
All inputs are finite; a program needn't handle non-finite values.
Results may differ from a plain program's by a relative error of at most 0.019.
Values may be sent and summed in bfloat16 or wider, within the bound.
A program may use at most 128 MiB of HBM per device.

v0:
```python
import functools
import types

import jax
import jax.numpy as jnp
from jax import lax
from jax.experimental import pallas as pl
from jax.experimental.pallas import tpu as pltpu
from jax.sharding import PartitionSpec as P

C_IN = 512
C_MID = 256
C_ATT = 128
C_OUT = 1024
H = 32
STEP = 4
MICRO = 2
MB = 3

EPSILON = 1e-05
HIGHEST = lax.Precision.HIGHEST
FLOAT = jnp.float32
BFLOAT = jnp.bfloat16
MESH = pl.DeviceIdType.MESH
LANES = 128
NIM = MICRO * MB
NN = (((1,), (0,)), ((), ()))
NT = (((1,), (1,)), ((), ()))
TN = (((0,), (0,)), ((), ()))


class Names:
    def __getattr__(self, name):
        return name


tag = Names()

SHAPES = dict(
    r1=(C_IN, C_MID),
    s1=(9 * C_MID, C_MID),
    q1=(C_MID, C_ATT),
    e1=(C_ATT, 2 * C_MID),
    o1=(C_MID, C_OUT),
    sh=(C_IN, C_OUT),
    r2=(C_OUT, C_MID),
    s2=(9 * C_MID, C_MID),
    q2=(C_MID, C_ATT),
    e2=(C_ATT, 2 * C_MID),
    o2=(C_MID, C_OUT),
)

HEIGHT, DP, ALL = range(3)
SYNCS = dict(
    n1=(16, C_MID // 2, ALL),
    n2=(8, C_MID, ALL),
    gap=(8, C_MID, HEIGHT),
    na=(8, C_ATT, DP),
    no=(16, C_OUT // 2, ALL),
    n1b=(8, C_MID // 2, ALL),
    n2b=(8, C_MID, ALL),
    gapb=(8, C_MID, HEIGHT),
    nab=(8, C_ATT, DP),
    nob=(8, C_OUT // 2, ALL),
    dnob=(8, C_OUT // 2, ALL),
    dattb=(8, 2 * C_MID, HEIGHT),
    dnab=(8, C_ATT, DP),
    dn2b=(8, C_MID, ALL),
    dn1b=(8, C_MID // 2, ALL),
    dno=(16, C_OUT // 2, ALL),
    datt=(8, 2 * C_MID, HEIGHT),
    dna=(8, C_ATT, DP),
    dn2=(8, C_MID, ALL),
    dn1=(16, C_MID // 2, ALL),
)
SEMAPHORES = 256
SMALL = dict(e2=0, q=16, e1=32)


def offsets():
    first = types.SimpleNamespace(
        reduce=0,
        split=C_MID,
        attend=3 * C_MID,
        output=3 * C_MID + C_ATT,
        shortcut=3 * C_MID + C_ATT + C_OUT,
    )
    base = 3 * C_MID + C_ATT + 2 * C_OUT
    second = types.SimpleNamespace(
        reduce=base,
        split=base + C_MID,
        attend=base + 3 * C_MID,
        output=base + 3 * C_MID + C_ATT,
    )
    total = base + 3 * C_MID + C_ATT + C_OUT
    first.bias = total
    second.bias = total + 2 * C_MID
    return (first, second)


GAIN_LEN = 6 * C_MID + 2 * C_ATT + 3 * C_OUT
SHIFT_LEN = GAIN_LEN + 4 * C_MID
GAIN_ROWS = 48
SHIFT_ROWS = 56


def stage_sizes(kind, nd, nh):
    if kind == HEIGHT:
        return (nh,)
    along = (nd,) if nd <= 8 else (8, nd // 8)
    return along if kind == DP else (nh,) + along


def row_table(per_device):
    table = {}
    at = 0
    parts = dict(
        r1=per_device[tag.r1],
        gs=16,
        s1=per_device[tag.s1],
        q=per_device[tag.q1] + per_device[tag.q2],
        e1=per_device[tag.e1],
        e2=per_device[tag.e2],
        o1=per_device[tag.o1],
        sh=per_device[tag.sh],
        r2=per_device[tag.r2],
        s2=per_device[tag.s2],
        o2=per_device[tag.o2],
    )
    for name, count in parts.items():
        table[name] = (at, count)
        at += count
    return table, at


def dot(left, right, dims=NN):
    return lax.dot_general(left, right, dims, preferred_element_type=FLOAT)


def exact(left, right, dims=NN):
    return lax.dot_general(left, right, dims, preferred_element_type=FLOAT, precision=HIGHEST)


def sigmoid(values):
    return 0.5 * jnp.tanh(0.5 * values) + 0.5


def slope_of(values):
    logistic = sigmoid(values)
    return logistic * (1.0 + values * (1.0 - logistic))


def widen(part, columns):
    return jnp.concatenate([part] * (columns // LANES), axis=1)


def fold(values):
    rows, columns = values.shape
    return jnp.sum(values.reshape(rows // 8, 8, columns), axis=0)


def iota(shape, axis):
    return lax.broadcasted_iota(jnp.int32, shape, axis)


def ones_where(condition, kind=BFLOAT):
    return jnp.where(condition, 1.0, 0.0).astype(FLOAT).astype(kind)


def shuffle(count, rows, blocks, back=False):
    new = iota((count, count), 1 if back else 0)
    old = iota((count, count), 0 if back else 1)
    hit = None
    for block in range(blocks):
        same = old == blocks * new - blocks * block * rows + block
        hit = same if hit is None else hit | same
    return hit


def kernel(cfg, names, *refs):
    R = types.SimpleNamespace(**dict(zip(names, refs)))
    nd, nh, inside = cfg.nd, cfg.nh, cfg.inside
    d, h = lax.axis_index(tag.dp), lax.axis_index(tag.height)
    first, second = offsets()
    used = [0]
    late = []
    share = 1.0 if inside else 1.0 / nh

    def new_sem():
        used[0] += 1
        assert used[0] <= SEMAPHORES
        return R.sem.at[used[0] - 1]

    def remote(source, target, send, receive, device):
        return pltpu.make_async_remote_copy(
            src_ref=source,
            dst_ref=target,
            send_sem=send,
            recv_sem=receive,
            device_id=device,
            device_id_type=MESH,
        )

    def wait_for(ref, sem):
        pltpu.make_async_copy(ref, ref, sem).wait()

    high = nd // 8 if nd > 8 else 1
    dp_low = (nd if nd <= 8 else 8, lax.div(d, high), lambda q: (q * high + lax.rem(d, high), h))
    dp_high = (high, lax.rem(d, high), lambda q: (lax.div(d, high) * high + q, h))
    dims_of = {
        HEIGHT: [(nh, h, lambda q: (d, q))],
        DP: [dp_low] + ([dp_high] if high > 1 else []),
    }
    dims_of[ALL] = dims_of[HEIGHT] + dims_of[DP]

    class Exchange:
        def __init__(self, name):
            self.stages = dims_of[SYNCS[name][2]]
            self.bufs = [getattr(R, "sy_" + name + str(k)) for k in range(len(self.stages))]

        def slot(self):
            return self.bufs[0].at[self.stages[0][1]]

        def send(self, stage):
            count, me, peer = self.stages[stage]
            buf = self.bufs[stage]
            send, self.receive = new_sem(), new_sem()
            for step in range(1, count):
                to = lax.rem(me + step, count)
                remote(buf.at[me], buf.at[me], send, self.receive, peer(to)).start()
            late.append(lambda: wait_for(buf.at[pl.ds(0, count - 1)], send))

        def start(self):
            self.send(0)

        def finish(self):
            total = None
            for stage, (count, me, _) in enumerate(self.stages):
                buf = self.bufs[stage]
                if total is not None:
                    buf[me] = total
                    self.send(stage)
                wait_for(buf.at[pl.ds(0, count - 1)], self.receive)
                total = buf[0]
                for other in range(1, count):
                    total = total + buf[other]
            return total

    def put(exchange, vectors):
        slot = exchange.slot()
        half = vectors[0].shape[1] // 2
        for at, vector in enumerate(vectors):
            slot[2 * at : 2 * at + 1, :] = vector[:, :half]
            slot[2 * at + 1 : 2 * at + 2, :] = vector[:, half:]

    def take(total, at):
        return jnp.concatenate([total[2 * at : 2 * at + 1], total[2 * at + 1 : 2 * at + 2]], axis=1)

    if inside:
        Z, X, Y, C = nd // 2, 2, nh // 2, 2
        z, x = lax.div(d, 2), lax.rem(d, 2)
        y, c = lax.div(h, 2), lax.rem(h, 2)
        table = cfg.table
        G = R.pack

        class Gather:
            def __init__(self, start, stop):
                self.rows = pl.ds(start, stop - start)
                self.phase = -1
                self.sends = []

            def part(self):
                rows = self.rows
                return [
                    G.at[pl.ds(0, Z - 1), x, y, c, rows],
                    G.at[:, x, y, c, rows],
                    G.at[:, :, y, c, rows],
                    G.at[:, :, :, c, rows],
                ][self.phase]

            def step(self):
                if self.phase >= 0:
                    wait_for(self.part(), self.receive)
                self.phase += 1
                if self.phase == 4:
                    return
                send, self.receive = new_sem(), new_sem()
                part = self.part()
                if self.phase == 0:
                    own = G.at[z, x, y, c, self.rows]
                    for step in range(1, Z):
                        to = lax.rem(z + step, Z)
                        remote(own, own, send, self.receive, (to * 2 + x, h)).start()
                else:
                    to = [(z * 2 + 1 - x, h), (d, (1 - y) * 2 + c), (d, y * 2 + 1 - c)][self.phase - 1]
                    remote(part, part, send, self.receive, to).start()
                self.sends.append(lambda: wait_for(part, send))

            def finish(self):
                while self.phase < 4:
                    self.step()

            def sent(self):
                for wait in self.sends:
                    wait()

        class Scatter:
            def __init__(self, start, stop):
                self.rows = pl.ds(start, stop - start)
                self.count = stop - start
                self.phase = -1

            def begin(self, source, target, to):
                send, self.receive = new_sem(), new_sem()
                remote(source, target, send, self.receive, to).start()
                late.append(lambda: wait_for(source, send))

            def step(self):
                rows = self.rows
                self.phase += 1
                if self.phase == 0:
                    self.begin(G.at[:, :, :, 1 - c, rows], R.rc.at[:, :, :, rows], (d, y * 2 + 1 - c))
                elif self.phase == 1:
                    wait_for(R.rc.at[:, :, :, rows], self.receive)

                    def add(zz, _):
                        for xx in range(X):
                            for yy in range(Y):
                                mine = G[zz, xx, yy, c, rows].astype(FLOAT)
                                G[zz, xx, yy, c, rows] = (
                                    mine + R.rc[zz, xx, yy, rows].astype(FLOAT)
                                ).astype(BFLOAT)
                        return 0

                    lax.fori_loop(0, Z, add, 0)
                    self.begin(G.at[:, :, 1 - y, c, rows], R.ry.at[:, :, rows], (d, (1 - y) * 2 + c))
                elif self.phase == 2:
                    wait_for(R.ry.at[:, :, rows], self.receive)

                    def add(zz, _):
                        for xx in range(X):
                            mine = G[zz, xx, y, c, rows].astype(FLOAT)
                            G[zz, xx, y, c, rows] = (mine + R.ry[zz, xx, rows].astype(FLOAT)).astype(
                                BFLOAT
                            )
                        return 0

                    lax.fori_loop(0, Z, add, 0)
                    self.begin(G.at[:, 1 - x, y, c, rows], R.rx.at[:, rows], (z * 2 + 1 - x, h))
                elif self.phase == 3:
                    wait_for(R.rx.at[:, rows], self.receive)

                    def add(zz, _):
                        mine = G[zz, x, y, c, rows].astype(FLOAT)
                        G[zz, x, y, c, rows] = (mine + R.rx[zz, rows].astype(FLOAT)).astype(BFLOAT)
                        return 0

                    lax.fori_loop(0, Z, add, 0)
                    send, self.receive = new_sem(), new_sem()
                    for step in range(1, Z):
                        to = lax.rem(z + step, Z)
                        remote(
                            G.at[to, x, y, c, rows], R.rz.at[z, rows], send, self.receive, (to * 2 + x, h)
                        ).start()
                    late.append(lambda: wait_for(R.rz.at[pl.ds(0, Z - 1), rows], send))
                elif self.phase == 4:
                    wait_for(R.rz.at[pl.ds(0, Z - 1), rows], self.receive)

            def finish(self):
                while self.phase < 4:
                    self.step()

        def scattered(name):
            start, count = table[name]
            rows = pl.ds(start, count)
            total = G[z, x, y, c, rows].astype(FLOAT)
            for step in range(1, Z):
                total = total + R.rz[lax.rem(z + step, Z), rows].astype(FLOAT)
            return total

        def own_rows(name, values):
            start, count = table[name]
            G[z, x, y, c, start : start + count] = values.astype(BFLOAT)

        def per_dev(name):
            return SHAPES[name][0] // (nd * nh)

        def pack_shards():
            for name in (tag.r1, tag.s1, tag.o1, tag.sh, tag.r2, tag.s2, tag.o2):
                rows, blocks = per_dev(name), SHAPES[name][1] // LANES
                order = ones_where(shuffle(rows * blocks, rows, blocks))
                own_rows(name, dot(order, getattr(R, "a_" + name)[...]))
            own_rows(tag.gs, R.gs[...])
            own_rows(
                "q", jnp.concatenate([R.a_q1[...].astype(FLOAT), R.a_q2[...].astype(FLOAT)], axis=0)
            )
            own_rows(tag.e1, R.a_e1[...])
            own_rows(tag.e2, R.a_e2[...])

        def unpack_rows(name):
            rows, blocks = per_dev(name), SHAPES[name][1] // LANES
            start = table[name][0]
            full = getattr(R, "w_" + name)
            for block in range(blocks):
                at = start + block * rows
                full[:, block * LANES : (block + 1) * LANES] = G[
                    :, :, :, :, at : at + rows, :
                ].reshape(nd * nh * rows, LANES)

        def unpack_pairs(name):
            blocks = SHAPES[name][1] // LANES
            start = table[name][0]
            full = getattr(R, "w_" + name)
            for pair in range(blocks // 2):
                at = start + 16 * pair
                both = G[:, :, :, :, at : at + 16, :].astype(FLOAT).reshape(nd * nh, 2, 8, LANES)
                for one in range(2):
                    block = 2 * pair + one
                    full[:, block * LANES : (block + 1) * LANES] = (
                        both[:, one].reshape(nd * nh * 8, LANES).astype(BFLOAT)
                    )

        def unpack_split(name):
            start, count = table[name]
            full = getattr(R, "w_" + name)
            rows = per_dev(name)
            group = nh * rows

            def body(j, _):
                zz, xx = lax.div(j, 2), lax.rem(j, 2)
                part = G[zz, xx, :, :, start : start + count, :].astype(FLOAT)
                part = part.reshape(nh, 2, rows, LANES)
                at = pl.ds(pl.multiple_of(j * group, group), group)
                for block in range(2):
                    full[at, block * LANES : (block + 1) * LANES] = (
                        part[:, block].reshape(group, LANES).astype(BFLOAT)
                    )
                return 0

            lax.fori_loop(0, nd, body, 0)

        def unpack_attention():
            at = table[tag.q][0]
            both = G[:, :, :, :, at : at + 16, :].astype(FLOAT).reshape(nd * nh, 2, 8, LANES)
            R.w_q1[...] = both[:, 0].reshape(C_MID, C_ATT)
            R.w_q2[...] = both[:, 1].reshape(C_MID, C_ATT)
            for name in (tag.e1, tag.e2):
                at = table[name][0]
                part = G[:, :, :, :, at : at + 16, :].reshape(4 * C_ATT, LANES)
                for block in range(4):
                    pick = ones_where(
                        iota((C_ATT, 4 * C_ATT), 1) == 4 * iota((C_ATT, 4 * C_ATT), 0) + block
                    )
                    getattr(R, "w_" + name)[:, block * LANES : (block + 1) * LANES] = dot(pick, part)

        def unpack_gains():
            at = table[tag.gs][0]
            part = G[:, :, :, :, at : at + 16, :].reshape(16 * nd * nh, LANES)
            for full, rows, first_row, length in (
                (R.gains, GAIN_ROWS, 0, GAIN_LEN // (nd * nh)),
                (R.shifts, SHIFT_ROWS, 3, SHIFT_LEN // (nd * nh)),
            ):
                shape = (rows, 16 * nd * nh)
                source = iota(shape, 1)
                row = (source & 15) - first_row
                target = (((source >> 4) * length) >> 7) + row
                hit = (row >= 0) & (row < 3) & (target == iota(shape, 0))
                full[...] = dot(ones_where(hit), part)

        def emit(name, at, values):
            start = table[name][0] if name[0] != "q" else 0
            rows = per_dev(name)
            if rows % 16 == 0:
                for block in range(values.shape[1] // LANES):
                    to = start + (at // LANES + block) * rows
                    part = values[:, block * LANES : (block + 1) * LANES].astype(BFLOAT)
                    G[:, :, :, :, to : to + rows, :] = part.reshape(Z, X, Y, C, rows, LANES)
            elif name[0] == "o":
                for pair in range(values.shape[1] // (2 * LANES)):
                    to = start + (at // LANES + 2 * pair) * 8
                    both = [
                        values[:, (2 * pair + one) * LANES : (2 * pair + one + 1) * LANES].reshape(
                            nd * nh, 8, LANES
                        )
                        for one in range(2)
                    ]
                    part = jnp.concatenate(both, axis=1).astype(BFLOAT)
                    G[:, :, :, :, to : to + 16, :] = part.reshape(Z, X, Y, C, 16, LANES)
            elif name[0] == "e":
                part = None
                for block in range(4):
                    place = ones_where(
                        iota((4 * C_ATT, C_ATT), 0) == 4 * iota((4 * C_ATT, C_ATT), 1) + block, FLOAT
                    )
                    term = exact(place, values[:, block * LANES : (block + 1) * LANES])
                    part = term if part is None else part + term
                at = SMALL[name]
                R.small[:, :, at : at + 16, :] = part.reshape(nd, nh, 16, LANES)
            elif name[0] == "q":
                getattr(R, "g_" + name)[...] = values

        def emit_squeezes():
            both = [part[...].reshape(nd * nh, 8, LANES) for part in (R.g_q1, R.g_q2)]
            part = jnp.concatenate(both, axis=1)
            at = SMALL[tag.q]
            R.small[:, :, at : at + 16, :] = part.reshape(nd, nh, 16, LANES)

        class SmallScatter:
            def __init__(self, start, count):
                self.rows = pl.ds(start, count)

            def start(self):
                send, self.receive = new_sem(), new_sem()
                rows = self.rows
                for step in range(1, nd):
                    to = lax.rem(d + step, nd)
                    source, target = R.small.at[to, h, rows], R.small_in.at[d, rows]
                    remote(source, target, send, self.receive, (to, h)).start()
                late.append(lambda: wait_for(R.small_in.at[pl.ds(0, nd - 1), rows], send))

            def finish(self):
                wait_for(R.small_in.at[pl.ds(0, nd - 1), self.rows], self.receive)
                total = R.small[d, h, self.rows]
                for step in range(1, nd):
                    total = total + R.small_in[lax.rem(d + step, nd), self.rows]
                return total

        def emit_split(name):
            start, count = table[name]
            rows = per_dev(name)
            group = nh * rows

            def body(j, _):
                zz, xx = lax.div(j, 2), lax.rem(j, 2)
                at = pl.ds(pl.multiple_of(j * group, group), group)
                both = [
                    R.grad[at, block * LANES : (block + 1) * LANES].reshape(nh, rows, LANES)
                    for block in range(2)
                ]
                part = jnp.concatenate(both, axis=1).astype(BFLOAT)
                G[zz, xx, :, :, start : start + count, :] = part.reshape(Y, C, count, LANES)
                return 0

            lax.fori_loop(0, nd, body, 0)

        def deliver(name):
            rows, blocks = per_dev(name), SHAPES[name][1] // LANES
            order = ones_where(shuffle(rows * blocks, rows, blocks, back=True), FLOAT)
            getattr(R, "d_" + name)[...] = exact(order, scattered(name))

        def range_of(*parts):
            return (table[parts[0]][0], table[parts[-1]][0] + table[parts[-1]][1])

        gathers = [
            Gather(*range_of(tag.r1, tag.gs)),
            Gather(*range_of(tag.s1)),
            Gather(*range_of(tag.q, tag.sh)),
            Gather(*range_of(tag.r2, tag.o2)),
        ]
        sums = dict(
            o2=Scatter(*range_of(tag.o2)),
            s2=Scatter(*range_of(tag.s2)),
            r2=Scatter(*range_of(tag.r2)),
            mid=Scatter(*range_of(tag.o1, tag.sh)),
            s1=Scatter(*range_of(tag.s1)),
            r1=Scatter(*range_of(tag.r1)),
        )
        small_two, small_one = SmallScatter(0, 16), SmallScatter(16, 32)
    else:

        def emit(name, at, values):
            getattr(R, "d_" + name)[:, at : at + values.shape[1]] = values

        def emit_split(name):
            getattr(R, "d_" + name)[...] = R.grad[...]

    def progress(which, steps=1):
        if inside:
            for _ in range(steps):
                which.step()

    def vector(ref, at, length):
        row = at // LANES
        return jnp.concatenate([ref[row + k : row + k + 1, :] for k in range(length // LANES)], axis=1)

    def store_vector(ref, at, values):
        row = at // LANES
        for k in range(values.shape[1] // LANES):
            ref[row + k : row + k + 1, :] = values[:, k * LANES : (k + 1) * LANES]

    def over_images(body):
        def step(i, _):
            body(i, lax.div(i, MB))
            return 0

        lax.fori_loop(0, NIM, step, 0)

    one = types.SimpleNamespace(
        suffix="", W=H, px=cfg.rows * H, hp=(cfg.rows + 2) * H, place=first, mk=R.mk1, edge=R.edge1, p1=R.p1,
        a3=R.a3, p2=R.p2, s=R.s, dp2=R.dp2, dmix=R.dmix, dy1=R.dmix, c1=R.c_n1, c2=R.c_n2, group=1,
        split=R.w_s1, squeeze=R.w_q1, expand=R.w_e1, att=R.att1, dgap=R.dgap1, count=0, keep=R.keep1, k="1",
    )
    two = types.SimpleNamespace(
        suffix="b", W=H // 2, px=cfg.rows * H // 4, hp=(cfg.rows // 2 + 2) * H // 2, place=second, mk=R.mk2,
        edge=R.edge2, p1=R.p1b, a3=R.a3b, p2=R.p2b, s=R.sb, dp2=R.dp2b, dmix=R.dmixb, dy1=R.dmixb,
        c1=R.c_n1b, c2=R.c_n2b, group=MB, split=R.w_s2, squeeze=R.w_q2, expand=R.w_e2, att=R.att2,
        dgap=R.dgap2, count=2, keep=R.keep2, k="2",
    )
    px1, px2 = one.px, two.px
    edge_rows = H

    def build_masks():
        for at, block in enumerate((one, two)):
            bits = block.W.bit_length() - 1
            shape = (block.hp, LANES)
            pixel = iota(shape, 0)
            column = pixel & (block.W - 1)
            place = iota(block.edge.shape[1:], 0) & (block.W - 1)
            block.edge[0] = ones_where(place != 0, FLOAT)
            block.edge[1] = ones_where(place != block.W - 1, FLOAT)
            row = (pixel >> bits) - 1 + h * (block.px // block.W)
            for i in range(NIM):
                limit = (H - STEP * (2 - R.groups[i])) // (1 if at == 0 else 2)
                inside_grid = (row >= 0) & (row < limit) & (column < limit)
                block.mk[i] = ones_where(inside_grid, FLOAT)

    def clear(ref):
        ref[...] = jnp.zeros(ref.shape, ref.dtype)

    def totals(kinds, columns):
        return [
            jnp.sum(R.acc[m, kind, :, :columns], axis=0, keepdims=True)
            for m in range(MICRO)
            for kind in range(kinds)
        ]

    def clear_acc(kinds, columns):
        for m in range(MICRO):
            for kind in range(kinds):
                R.acc[m, kind, :, :columns] = jnp.zeros((8, columns), FLOAT)

    def chunk_of(columns):
        return 32 if columns <= 512 else 16

    def stat_pass(source, start, px, columns, mk, mask_start):
        chunk = chunk_of(columns)
        clear_acc(2, columns)

        def body(i, m):
            total, square = R.acc[m, 0, :, :columns], R.acc[m, 1, :, :columns]
            for t in range(0, px, chunk):
                v = source[i, start + t : start + t + chunk, :]
                vm = v * widen(mk[i, mask_start + t : mask_start + t + chunk, :], columns)
                total = total + fold(vm)
                square = square + fold(vm * v)
            R.acc[m, 0, :, :columns] = total
            R.acc[m, 1, :, :columns] = square

        over_images(body)
        return totals(2, columns)

    def inverse_count(block, m, columns):
        return widen(R.counts[block.count + m : block.count + m + 1, :], columns)

    def norm_coef(coef, total, at, columns, block, offset):
        gain, shift = vector(R.gains, offset, columns), vector(R.shifts, offset, columns)
        for m in range(MICRO):
            inverse = inverse_count(block, m, columns)
            centre = take(total, at + 2 * m) * inverse
            scaled = lax.rsqrt(take(total, at + 2 * m + 1) * inverse - centre * centre + EPSILON)
            coef[m, 0:1, :] = gain * scaled
            coef[m, 1:2, :] = shift - centre * (gain * scaled)
            coef[m, 2:3, :] = scaled
            coef[m, 3:4, :] = -centre * scaled

    def norm_coef_back(coef, total, pairs, columns, block, offset):
        for m, (at_sum, at_along) in enumerate(pairs):
            inverse = inverse_count(block, m, columns)
            summed, along = take(total, at_sum), take(total, at_along)
            scale = -coef[m, 0:1, :] * inverse
            coef[m, 4:5, :] = scale * (summed + along * coef[m, 3:4, :])
            coef[m, 5:6, :] = scale * along * coef[m, 2:3, :]
        sums_ = [take(total, pair[0]) for pair in pairs]
        alongs = [take(total, pair[1]) for pair in pairs]
        store_vector(R.all_shifts, offset, sums_[0] + sums_[1])
        store_vector(R.all_gains, offset, alongs[0] + alongs[1])

    class Halo:
        def __init__(self, down=None, up=None):
            self.ways = []
            for pair, step in ((down, 1), (up, -1)):
                if pair is not None:
                    sends = h < nh - 1 if step == 1 else h > 0
                    gets = h > 0 if step == 1 else h < nh - 1
                    copy = remote(pair[0], pair[1], new_sem(), new_sem(), (d, h + step))
                    self.ways.append((sends, gets, copy))

        def start(self):
            for sends, _, copy in self.ways:
                pl.when(sends)(copy.start)

        def finish(self):
            for _, gets, copy in self.ways:
                pl.when(gets)(copy.wait_recv)
            late.append(self.sent)

        def sent(self):
            for sends, _, copy in self.ways:
                pl.when(sends)(copy.wait_send)
            self.ways = []

    def activate(block):
        half = C_MID // 2

        def body(i, m):
            mask = block.mk[i]
            for g in range(2):
                cols = slice(g * half, (g + 1) * half)
                value = block.c1[m, 0:1, cols] * block.p1[i, :, cols] + block.c1[m, 1:2, cols]
                value = value * sigmoid(value) * mask
                if block is one:
                    R.a_sum[:, cols] = R.a_sum[:, cols] + fold(value[block.W : block.W + block.px])
                at = 3 * g * half
                left = pltpu.roll(value, 1, 0) * block.edge[0, : block.hp]
                right = pltpu.roll(value, block.hp - 1, 0) * block.edge[1, : block.hp]
                block.a3[i, :, at : at + half] = left.astype(BFLOAT)
                block.a3[i, :, at + half : at + 2 * half] = value.astype(BFLOAT)
                block.a3[i, :, at + 2 * half : at + 3 * half] = right.astype(BFLOAT)

        over_images(body)

    def in_groups(block, body):
        if block.group == 1:
            over_images(lambda i, m: body(i, 1, m))
        else:
            for m in range(MICRO):
                body(m * MB, MB, m)

    def rows_of(ref, i, count, start, rows, cols):
        part = ref[pl.ds(i, count), start : start + rows, cols]
        return part.reshape(count * rows, part.shape[-1])

    def convolve(block):
        half = C_MID // 2

        def body(i, count, m):
            for g in range(2):
                cols = slice(3 * g * half, 3 * (g + 1) * half)
                taps = [rows_of(block.a3, i, count, dy * block.W, block.px, cols) for dy in range(3)]
                matrix = block.split[9 * g * half : 9 * (g + 1) * half, :]
                result = dot(jnp.concatenate(taps, axis=1), matrix)
                block.p2[pl.ds(i, count), :, g * C_MID : (g + 1) * C_MID] = result.reshape(
                    count, block.px, C_MID
                )

        in_groups(block, body)

    def split_activate(block):
        columns = 2 * C_MID

        def body(i, m):
            gap = jnp.zeros((8, C_MID), FLOAT)
            for t in range(0, block.px, 32):
                at = slice(t, t + 32)
                mask = widen(block.mk[i, block.W + t : block.W + t + 32, :], columns)
                value = block.c2[m, 0:1, :] * block.p2[i, at, :] + block.c2[m, 1:2, :]
                value = value * sigmoid(value) * mask
                block.s[i, at, :] = value
                gap = gap + fold(value[:, :C_MID] + value[:, C_MID:])
            R.image_sums[i, :, :C_MID] = gap

        over_images(body)

    def put_image_sums(exchange, columns):
        slot = exchange.slot()
        for i in range(NIM):
            slot[i : i + 1, :] = jnp.sum(R.image_sums[i, :, :columns], axis=0, keepdims=True)
        slot[NIM:8, :] = jnp.zeros((8 - NIM, columns), FLOAT)

    def micro_sums(values):
        row = iota(values.shape, 0)
        return [
            jnp.sum(
                jnp.where((row >= m * MB) & (row < (m + 1) * MB), values, 0.0), axis=0, keepdims=True
            )
            for m in range(MICRO)
        ]

    def micro_pick(vectors, rows=8):
        shape = (rows, vectors[0].shape[1])
        return jnp.where(
            iota(shape, 0) < MB, jnp.broadcast_to(vectors[0], shape), jnp.broadcast_to(vectors[1], shape)
        )

    def inverse_area(block):
        shape = (8, C_MID)
        row = iota(shape, 0)
        side = jnp.ones(shape, FLOAT)
        for i in range(NIM):
            limit = (H - STEP * (2 - R.groups[i])) // (1 if block is one else 2)
            side = jnp.where(row == i, limit.astype(FLOAT), side)
        return 1.0 / (side * side)

    def attend(block, window_gap, window_norm):
        suffix = block.suffix
        gap, norm = Exchange(tag.gap + suffix), Exchange(tag.na + suffix)
        split_activate(block)
        put_image_sums(gap, C_MID)
        gap.start()
        window_gap()
        keep = block.keep
        pooled = gap.finish() * inverse_area(block)
        keep[0, :, :C_MID] = pooled
        before = exact(pooled, block.squeeze[...])
        firsts, seconds = micro_sums(before), micro_sums(before * before)
        slot = norm.slot()
        for m in range(MICRO):
            slot[2 * m : 2 * m + 1, :] = firsts[m]
            slot[2 * m + 1 : 2 * m + 2, :] = seconds[m]
        slot[4:8, :] = jnp.zeros((4, C_ATT), FLOAT)
        norm.start()
        window_norm()
        total = norm.finish()
        count = MB * nd
        centres, scales = [], []
        for m in range(MICRO):
            centre = total[2 * m : 2 * m + 1] / count
            centres.append(centre)
            scales.append(
                lax.rsqrt(total[2 * m + 1 : 2 * m + 2] / count - centre * centre + EPSILON)
            )
        scale = micro_pick(scales)
        normal = (before - micro_pick(centres)) * scale
        gain = vector(R.gains, block.place.attend, C_ATT)
        shift = vector(R.shifts, block.place.attend, C_ATT)
        normed = gain * normal + shift
        hidden = normed * sigmoid(normed)
        keep[1, :, :C_ATT] = normal
        keep[2, :, :C_ATT] = normed
        keep[3, :, :C_ATT] = hidden
        keep[4, :, :C_ATT] = gain * scale
        logits = exact(hidden, block.expand[...]) + vector(R.shifts, block.place.bias, 2 * C_MID)
        gap_logit = logits[:, :C_MID] - logits[:, C_MID:]
        keep[5, :, :] = jnp.concatenate([sigmoid(gap_logit), sigmoid(-gap_logit)], axis=1)
        for i in range(NIM):
            block.att[i] = jnp.broadcast_to(keep[5, i : i + 1, :], (8, 2 * C_MID))

    def mix(block, target, start):
        def body(i, m):
            for t in range(0, block.px, 32):
                at = slice(t, t + 32)
                value = (
                    block.att[i, 0:1, :C_MID] * block.s[i, at, :C_MID]
                    + block.att[i, 0:1, C_MID:] * block.s[i, at, C_MID:]
                )
                target[i, start + t : start + t + 32, :] = value.astype(BFLOAT)

        over_images(body)

    def attend_back(block, window_att, window_norm):
        suffix = block.suffix

        def body(i, m):
            parts = [jnp.zeros((8, C_MID), FLOAT)] * 2
            for t in range(0, block.px, 32):
                at = slice(t, t + 32)
                grad = block.dmix[i, at, :]
                for j in range(2):
                    parts[j] = parts[j] + fold(grad * block.s[i, at, j * C_MID : (j + 1) * C_MID])
            R.image_sums[i] = jnp.concatenate(parts, axis=1)

        over_images(body)
        heights, norm = Exchange(tag.datt + suffix), Exchange(tag.dna + suffix)
        put_image_sums(heights, 2 * C_MID)
        heights.start()
        window_att()
        grad_att = heights.finish()
        keep = block.keep
        att = keep[5]
        weighted = att * grad_att
        both = weighted[:, :C_MID] + weighted[:, C_MID:]
        grad_logits = weighted - att * jnp.concatenate([both, both], axis=1)
        grad_hidden = exact(grad_logits, block.expand[...], NT)
        grad_normed = grad_hidden * slope_of(keep[2, :, :C_ATT])
        normal = keep[1, :, :C_ATT]
        firsts, seconds = micro_sums(grad_normed), micro_sums(grad_normed * normal)
        bias = jnp.sum(grad_logits, axis=0, keepdims=True)
        slot = norm.slot()
        for m in range(MICRO):
            slot[2 * m : 2 * m + 1, :] = firsts[m]
            slot[2 * m + 1 : 2 * m + 2, :] = seconds[m]
        for k in range(4):
            slot[4 + k : 5 + k, :] = bias[:, k * LANES : (k + 1) * LANES]
        norm.start()
        emit(tag.e + block.k, 0, exact(keep[3, :, :C_ATT], grad_logits, TN) * share)
        window_norm()
        total = norm.finish()
        count = MB * nd
        store_vector(R.all_shifts, block.place.attend, total[0:1] + total[2:3])
        store_vector(R.all_gains, block.place.attend, total[1:2] + total[3:4])
        for k in range(4):
            store_vector(R.all_shifts, block.place.bias + k * LANES, total[4 + k : 5 + k])
        summed = micro_pick([total[0:1], total[2:3]])
        along = micro_pick([total[1:2], total[3:4]])
        grad_before = keep[4, :, :C_ATT] * (grad_normed - (summed + normal * along) / count)
        grad_gap = exact(grad_before, block.squeeze[...], NT) * inverse_area(block)
        for i in range(NIM):
            block.dgap[i] = jnp.broadcast_to(grad_gap[i : i + 1, :], (8, C_MID))
        emit(tag.q + block.k, 0, exact(keep[0, :, :C_MID], grad_before, TN) * share)

    def split_back(block):
        clear_acc(2, 2 * C_MID)

        def body(i, m):
            for j in range(2):
                cols = slice(j * C_MID, (j + 1) * C_MID)
                total, along = R.acc[m, 0, :, cols], R.acc[m, 1, :, cols]
                for t in range(0, block.px, 32):
                    at = slice(t, t + 32)
                    mask = widen(block.mk[i, block.W + t : block.W + t + 32, :], C_MID)
                    raw = block.p2[i, at, cols]
                    value = block.c2[m, 0:1, cols] * raw + block.c2[m, 1:2, cols]
                    grad = block.att[i, 0:1, cols] * block.dmix[i, at, :] + block.dgap[i, 0:1, :]
                    grad = grad * slope_of(value) * mask
                    block.s[i, at, cols] = grad
                    total = total + fold(grad)
                    along = along + fold(
                        grad * (block.c2[m, 2:3, cols] * raw + block.c2[m, 3:4, cols])
                    )
                R.acc[m, 0, :, cols] = total
                R.acc[m, 1, :, cols] = along

        over_images(body)

    def norm_back(block_px, grad, coef, raw, raw_start, mk, mask_start, target, start, columns):
        chunk = chunk_of(columns)

        def body(i, m):
            for t in range(0, block_px, chunk):
                mask = widen(mk[i, mask_start + t : mask_start + t + chunk, :], columns)
                value = (
                    coef[m, 0:1, :] * grad[i, t : t + chunk, :]
                    + coef[m, 4:5, :]
                    + coef[m, 5:6, :] * raw[i, raw_start + t : raw_start + t + chunk, :]
                )
                target[i, start + t : start + t + chunk, :] = (value * mask).astype(BFLOAT)

        over_images(body)

    def product_of_means(g):
        half = C_MID // 2
        eye = iota((half, half), 0) == iota((half, half), 1)
        row = jnp.broadcast_to(R.centre[0:1, g * half : (g + 1) * half], (half, half))
        column = jnp.sum(jnp.where(eye, row, 0.0), axis=1, keepdims=True)
        return column * R.grad_sum[0:1, g * C_MID : (g + 1) * C_MID]

    def mean_term():
        half = C_MID // 2
        rows = SHAPES[tag.s1][0] // (nd * nh)
        index = d * nh + h
        low = index * rows < 9 * half
        centre = jnp.where(low, R.centre[0:1, :half], R.centre[0:1, half:])
        sums_ = jnp.where(low, R.grad_sum[1:2, :C_MID], R.grad_sum[1:2, C_MID:])
        shape = (2 * rows, LANES)
        row = iota(shape, 0)
        hit = iota(shape, 1) == ((index * rows + (row >> 1)) & (half - 1))
        column = jnp.sum(
            jnp.where(hit, jnp.broadcast_to(centre, shape), 0.0), axis=1, keepdims=True
        )
        odd = (row & 1) == 1
        return column * jnp.where(
            odd, jnp.broadcast_to(sums_[:, LANES:], shape), jnp.broadcast_to(sums_[:, :LANES], shape)
        )

    def kernel_grad(block, g):
        half = C_MID // 2
        images = MB if block.group == 1 else NIM
        for dy in range(3):
            at = slice(9 * g * half + 3 * dy * half, 9 * g * half + 3 * (dy + 1) * half)
            total = None
            for i in range(0, NIM, images):
                taps = rows_of(
                    block.a3, i, images, dy * block.W, block.px, slice(3 * g * half, 3 * (g + 1) * half)
                )
                grad = rows_of(
                    block.dp2, i, images, block.W, block.px, slice(g * C_MID, (g + 1) * C_MID)
                )
                term = dot(taps, grad, TN)
                total = term if total is None else total + term
            if inside and block is one:
                total = total - jnp.concatenate([product_of_means(g)] * 3, axis=0)
            R.grad[at, :] = total

    def convolve_back(block):
        half = C_MID // 2
        clear_acc(2, C_MID)

        def body(i, count, m):
            rows = count * block.px
            for g in range(2):
                cols = slice(g * half, (g + 1) * half)
                total = None
                for dy in range(3):
                    grad = rows_of(
                        block.dp2, i, count, (2 - dy) * block.W, block.px, slice(g * C_MID, (g + 1) * C_MID)
                    )
                    at = 9 * g * half + 3 * dy * half
                    term = dot(grad, block.split[at : at + 3 * half, :], NT)
                    total = term if total is None else total + term
                value = (
                    total[:, half : 2 * half]
                    + pltpu.roll(total[:, :half], rows - 1, 0) * block.edge[1, :rows]
                    + pltpu.roll(total[:, 2 * half :], 1, 0) * block.edge[0, :rows]
                )
                raw = rows_of(block.p1, i, count, block.W, block.px, cols)
                mask = rows_of(block.mk, i, count, block.W, block.px, slice(0, LANES))
                before = block.c1[m, 0:1, cols] * raw + block.c1[m, 1:2, cols]
                value = value * slope_of(before) * mask
                block.dy1[pl.ds(i, count), :, cols] = value.reshape(count, block.px, half)
                normal = block.c1[m, 2:3, cols] * raw + block.c1[m, 3:4, cols]
                R.acc[m, 0, :, cols] = R.acc[m, 0, :, cols] + fold(value)
                R.acc[m, 1, :, cols] = R.acc[m, 1, :, cols] + fold(value * normal)

        in_groups(block, body)

    def sum_gradients(i, m):
        total = jnp.where(i == 0, 0.0, R.acc[0, 2, :, : 2 * C_MID])
        for t in range(0, one.px, 32):
            total = total + fold(R.dp2[i, one.W + t : one.W + t + 32, :].astype(FLOAT))
        R.acc[0, 2, :, : 2 * C_MID] = total

    def splat_back(block, halo, window_att, window_norm, window_split, window_reduce):
        suffix = block.suffix
        attend_back(block, window_att, window_norm)
        split_back(block)
        exchange = Exchange(tag.dn2 + suffix)
        put(exchange, totals(2, 2 * C_MID))
        exchange.start()
        window_split()
        norm_coef_back(
            block.c2, exchange.finish(), ((0, 1), (2, 3)), 2 * C_MID, block, block.place.split
        )
        norm_back(
            block.px, block.s, block.c2, block.p2, 0, block.mk, block.W, block.dp2, block.W, 2 * C_MID
        )
        halo.start()
        if block is one:
            over_images(sum_gradients)
            R.grad_sum[0:1, :] = jnp.sum(R.acc[0, 2, :, : 2 * C_MID], axis=0, keepdims=True)
        kernel_grad(block, 0)
        halo.finish()
        convolve_back(block)
        exchange = Exchange(tag.dn1 + suffix)
        put(exchange, totals(2, C_MID))
        if block is one:
            slot = exchange.slot()
            for k in range(4):
                slot[8 + k : 9 + k, :] = R.grad_sum[0:1, k * LANES : (k + 1) * LANES]
            slot[12:16, :] = jnp.zeros((4, LANES), FLOAT)
        exchange.start()
        kernel_grad(block, 1)
        emit_split(tag.s + block.k)
        window_reduce()
        total = exchange.finish()
        if block is one:
            for k in range(4):
                R.grad_sum[1:2, k * LANES : (k + 1) * LANES] = total[8 + k : 9 + k]
        norm_coef_back(block.c1, total, ((0, 1), (2, 3)), C_MID, block, block.place.reduce)
        norm_back(
            block.px, block.dy1, block.c1, block.p1, block.W, block.mk, block.W, block.dp1, 0, C_MID
        )

    one.dp1, two.dp1 = R.dp1, R.dp1b
    halo_x = Halo(
        (R.images.at[:, pl.ds(px1 - edge_rows, edge_rows)], R.xh.at[:, pl.ds(0, edge_rows)]),
        (R.images.at[:, pl.ds(0, edge_rows)], R.xh.at[:, pl.ds(one.hp - edge_rows, edge_rows)]),
    )
    load_x = pltpu.make_async_copy(R.images, R.xh.at[:, pl.ds(edge_rows, px1)], new_sem())
    load_cot = pltpu.make_async_copy(R.cotangent, R.cot, new_sem())
    load_x.start()
    load_cot.start()
    for block, refs_ in (
        (one, (R.xh, R.dp2)),
        (two, (R.p1b, R.dp2b)),
    ):
        for ref in refs_:
            shape = (NIM, block.W, ref.shape[-1])
            ref[:, : block.W, :] = jnp.zeros(shape, ref.dtype)
            ref[:, block.hp - block.W :, :] = jnp.zeros(shape, ref.dtype)
    clear(R.a_sum)
    R.v1[:, :edge_rows, :] = jnp.zeros((NIM, edge_rows, C_MID), BFLOAT)
    R.dq[:, px2:, :] = jnp.zeros((NIM, two.W, C_MID), BFLOAT)

    barrier = pltpu.get_barrier_semaphore()
    partners = 0
    for step in range(1, nh):
        to = (d, lax.rem(h + step, nh))
        pl.semaphore_signal(barrier, inc=1, device_id=to, device_id_type=MESH)
        partners += 1
    if high == 1:
        for step in range(1, nd):
            to = (lax.rem(d + step, nd), h)
            pl.semaphore_signal(barrier, inc=1, device_id=to, device_id_type=MESH)
            partners += 1
    else:
        for count, me, peer in dims_of[DP]:
            for step in range(1, count):
                to = peer(lax.rem(me + step, count))
                pl.semaphore_signal(barrier, inc=1, device_id=to, device_id_type=MESH)
                partners += 1
    if inside:
        pack_shards()
    pl.semaphore_wait(barrier, partners)

    if inside:
        gathers[0].step()
    halo_x.start()
    if inside:
        for gather in gathers[1:]:
            gather.step()
    build_masks()

    out_shape = (px2, px1 + edge_rows)
    out_pixel, in_pixel = iota(out_shape, 0), iota(out_shape, 1)
    down = (in_pixel >> 5) - 2 * (out_pixel >> 4)
    along_ = (in_pixel & 31) - 2 * (out_pixel & 15) + 1
    R.pool3[...] = ones_where((down >= 0) & (down < 3) & (along_ >= 0) & (along_ < 3))
    out_shape = (px2, px1)
    out_pixel, in_pixel = iota(out_shape, 0), iota(out_shape, 1)
    cell = ((in_pixel >> 6) == (out_pixel >> 4)) & (((in_pixel & 31) >> 1) == (out_pixel & 15))
    R.pool2[...] = jnp.where(cell, 0.25, 0.0).astype(FLOAT).astype(BFLOAT)
    back_shape = (px1, px2)
    in_pixel, out_pixel = iota(back_shape, 0), iota(back_shape, 1)
    cell = ((in_pixel >> 6) == (out_pixel >> 4)) & (((in_pixel & 31) >> 1) == (out_pixel & 15))
    R.spread2[...] = jnp.where(cell, 0.25, 0.0).astype(FLOAT).astype(BFLOAT)
    back_shape = (px1, px2 + two.W)
    in_pixel, out_pixel = iota(back_shape, 0), iota(back_shape, 1)
    down = (in_pixel >> 5) + 1 - 2 * (out_pixel >> 4)
    along_ = (in_pixel & 31) + 1 - 2 * (out_pixel & 15)
    R.spread3[...] = ones_where((down >= 0) & (down < 3) & (along_ >= 0) & (along_ < 3))

    if inside:
        gathers[0].finish()
        unpack_rows(tag.r1)
        unpack_gains()
    load_x.wait()
    halo_x.finish()

    def body(i, m):
        R.p1[i] = dot(R.xh[i], R.w_r1[...])

    over_images(body)
    if inside:
        gathers[1].step()
    exchange = Exchange(tag.n1)
    put(exchange, stat_pass(R.p1, one.W, px1, C_MID, R.mk1, one.W))
    slot = exchange.slot()
    for m in range(MICRO):
        cells = jnp.zeros((8, LANES), FLOAT)
        for i in range(m * MB, (m + 1) * MB):
            cells = cells + fold(R.mk1[i, one.W : one.W + px1, :])
        slot[8 + m : 9 + m, :] = jnp.sum(cells, axis=0, keepdims=True)
    slot[10:16, :] = jnp.zeros((6, LANES), FLOAT)
    exchange.start()
    if inside:
        gathers[1].step()

    def body(i, m):
        R.t1[i] = dot(R.pool2[...], R.xh[i, edge_rows : edge_rows + px1, :]).astype(BFLOAT)

    over_images(body)
    total = exchange.finish()
    for m in range(MICRO):
        R.counts[m : m + 1, :] = 1.0 / total[8 + m : 9 + m, :]
        R.counts[2 + m : 3 + m, :] = 4.0 / total[8 + m : 9 + m, :]
    norm_coef(R.c_n1, total, 0, C_MID, one, first.reduce)
    if inside:
        gathers[1].step()
        gathers[2].step()
    activate(one)
    if inside:
        gathers[1].finish()
        unpack_split(tag.s1)
    convolve(one)
    exchange = Exchange(tag.n2)
    put(exchange, stat_pass(R.p2, 0, px1, 2 * C_MID, R.mk1, one.W))
    exchange.start()
    if inside:
        gathers[2].step()
        gathers[3].step()
    norm_coef(R.c_n2, exchange.finish(), 0, 2 * C_MID, one, first.split)
    if inside:
        gathers[2].step()

    def window_gap():
        if inside:
            gathers[2].finish()
            unpack_attention()

    def window_norm():
        if inside:
            gathers[3].step()
            unpack_rows(tag.sh)
            unpack_pairs(tag.o1)

    attend(one, window_gap, window_norm)
    mix(one, R.v1, edge_rows)
    halo_v = Halo((R.v1.at[:, pl.ds(px1, edge_rows)], R.v1.at[:, pl.ds(0, edge_rows)]))
    halo_v.start()

    def outer(ref, columns):
        return ref[...].reshape(NIM * px2, columns)

    def product_out(source, inner, matrix, target):
        for at in range(0, C_OUT, 256):
            target[:, :, at : at + 256] = dot(outer(source, inner), matrix[:, at : at + 256]).reshape(
                NIM, px2, 256
            )

    product_out(R.t1, C_IN, R.w_sh, R.csh)
    exchange = Exchange(tag.no)
    stats_short = stat_pass(R.csh, 0, px2, C_OUT, R.mk2, two.W)
    halo_v.finish()

    def body(i, m):
        R.q1[i] = (dot(R.pool3[...], R.v1[i]) * (1.0 / 9.0)).astype(BFLOAT)

    over_images(body)
    product_out(R.q1, C_MID, R.w_o1, R.o1)
    put(exchange, stat_pass(R.o1, 0, px2, C_OUT, R.mk2, two.W) + stats_short)
    exchange.start()
    if inside:
        gathers[3].finish()
        unpack_rows(tag.r2)
        unpack_split(tag.s2)
        unpack_pairs(tag.o2)
    total = exchange.finish()
    norm_coef(R.c_o1, total, 0, C_OUT, two, first.output)
    norm_coef(R.c_sh, total, 4, C_OUT, two, first.shortcut)

    def first_sum(i, m, at, mask_rows):
        return (
            R.c_o1[m, 0:1, :] * R.o1[i, at, :]
            + R.c_sh[m, 0:1, :] * R.csh[i, at, :]
            + (R.c_o1[m, 1:2, :] + R.c_sh[m, 1:2, :])
        )

    def body(i, m):
        for t in range(0, px2, 16):
            at = slice(t, t + 16)
            value = first_sum(i, m, at, None)
            mask = widen(R.mk2[i, two.W + t : two.W + t + 16, :], C_OUT)
            R.l1[i, at, :] = (value * sigmoid(value) * mask).astype(BFLOAT)

    over_images(body)
    store_one = pltpu.make_async_copy(R.l1, R.layer_one, new_sem())
    store_one.start()
    late.append(store_one.wait)

    R.p1b[:, two.W : two.W + px2, :] = dot(outer(R.l1, C_OUT), R.w_r2[...]).reshape(
        NIM, px2, C_MID
    )
    halo_p = Halo(
        (R.p1b.at[:, pl.ds(px2, two.W)], R.p1b.at[:, pl.ds(0, two.W)]),
        (R.p1b.at[:, pl.ds(two.W, two.W)], R.p1b.at[:, pl.ds(two.hp - two.W, two.W)]),
    )
    exchange = Exchange(tag.n1b)
    put(exchange, stat_pass(R.p1b, two.W, px2, C_MID, R.mk2, two.W))
    exchange.start()
    halo_p.start()
    norm_coef(R.c_n1b, exchange.finish(), 0, C_MID, two, second.reduce)
    halo_p.finish()
    activate(two)
    convolve(two)
    exchange = Exchange(tag.n2b)
    put(exchange, stat_pass(R.p2b, 0, px2, 2 * C_MID, R.mk2, two.W))
    exchange.start()
    norm_coef(R.c_n2b, exchange.finish(), 0, 2 * C_MID, two, second.split)
    attend(two, lambda: None, lambda: None)
    mix(two, R.mix2, 0)
    product_out(R.mix2, C_MID, R.w_o2, R.o2)
    exchange = Exchange(tag.nob)
    put(exchange, stat_pass(R.o2, 0, px2, C_OUT, R.mk2, two.W))
    exchange.start()
    load_cot.wait()
    norm_coef(R.c_o2, exchange.finish(), 0, C_OUT, two, second.output)

    clear_acc(2, C_OUT)

    def body(i, m):
        total, along = R.acc[m, 0], R.acc[m, 1]
        for t in range(0, px2, 16):
            at = slice(t, t + 16)
            mask = widen(R.mk2[i, two.W + t : two.W + t + 16, :], C_OUT)
            raw = R.o2[i, at, :]
            value = R.c_o2[m, 0:1, :] * raw + R.c_o2[m, 1:2, :] + R.l1[i, at, :].astype(FLOAT)
            logistic = sigmoid(value)
            R.dpo[i, at, :] = (value * logistic * mask).astype(BFLOAT)
            grad = R.cot[i, at, :].astype(FLOAT) * mask * (logistic * (1.0 + value * (1.0 - logistic)))
            R.g2[i, at, :] = grad
            total = total + fold(grad)
            along = along + fold(grad * (R.c_o2[m, 2:3, :] * raw + R.c_o2[m, 3:4, :]))
        R.acc[m, 0] = total
        R.acc[m, 1] = along

    over_images(body)
    exchange = Exchange(tag.dnob)
    put(exchange, totals(2, C_OUT))
    exchange.start()
    store_two = pltpu.make_async_copy(R.dpo, R.layer_two, new_sem())
    store_two.start()
    norm_coef_back(R.c_o2, exchange.finish(), ((0, 1), (2, 3)), C_OUT, two, second.output)
    store_two.wait()
    norm_back(px2, R.g2, R.c_o2, R.o2, 0, R.mk2, two.W, R.dpo, 0, C_OUT)
    R.dmixb[...] = dot(outer(R.dpo, C_OUT), R.w_o2[...], NT).reshape(NIM, px2, C_MID)

    def grad_outer(name, source, inner, grad):
        for at in range(0, C_OUT, 256):
            part = grad[:, :, at : at + 256].reshape(NIM * px2, 256)
            emit(name, at, dot(outer(source, inner), part, TN))

    def window_att():
        if inside:
            for gather in gathers:
                gather.sent()
        grad_outer(tag.o2, R.mix2, C_MID, R.dpo)
        if inside:
            sums[tag.o2].step()

    def window_norm():
        if inside:
            sums[tag.o2].step()

    def window_split():
        if inside:
            sums[tag.o2].step()
            small_two.start()

    def window_reduce():
        if inside:
            sums[tag.o2].step()
            sums[tag.s2].step()

    halo_d = Halo(
        (R.dp2b.at[:, pl.ds(px2, two.W)], R.dp2b.at[:, pl.ds(0, two.W)]),
        (R.dp2b.at[:, pl.ds(two.W, two.W)], R.dp2b.at[:, pl.ds(two.hp - two.W, two.W)]),
    )
    splat_back(two, halo_d, window_att, window_norm, window_split, window_reduce)

    clear_acc(3, C_OUT)
    R.o2[...] = dot(outer(R.dp1b, C_MID), R.w_r2[...], NT).reshape(NIM, px2, C_OUT)

    def body(i, m):
        sums_ = [R.acc[m, kind] for kind in range(3)]
        for t in range(0, px2, 16):
            at = slice(t, t + 16)
            mask = widen(R.mk2[i, two.W + t : two.W + t + 16, :], C_OUT)
            value = first_sum(i, m, at, None)
            grad = (R.g2[i, at, :] + R.o2[i, at, :]) * mask * slope_of(value)
            R.g2[i, at, :] = grad
            sums_[0] = sums_[0] + fold(grad)
            sums_[1] = sums_[1] + fold(
                grad * (R.c_o1[m, 2:3, :] * R.o1[i, at, :] + R.c_o1[m, 3:4, :])
            )
            sums_[2] = sums_[2] + fold(
                grad * (R.c_sh[m, 2:3, :] * R.csh[i, at, :] + R.c_sh[m, 3:4, :])
            )
        for kind in range(3):
            R.acc[m, kind] = sums_[kind]

    over_images(body)
    exchange = Exchange(tag.dno)
    put(exchange, totals(3, C_OUT))
    slot = exchange.slot()
    slot[12:16, :] = jnp.zeros((4, C_OUT // 2), FLOAT)
    slot[12:13, :C_MID] = jnp.sum(R.a_sum[...], axis=0, keepdims=True)
    exchange.start()
    if inside:
        sums[tag.o2].step()
        sums[tag.s2].step()
    dp1b = outer(R.dp1b, C_MID)
    for at in range(0, C_MID, 128):
        emit(tag.r2, at, dot(outer(R.l1, C_OUT), dp1b[:, at : at + 128], TN))
    if inside:
        sums[tag.r2].step()
    total = exchange.finish()
    counts = R.counts[0:1, :], R.counts[1:2, :]
    R.centre[0:1, :] = total[12:13, :C_MID] * widen(
        counts[0] * counts[1] / (counts[0] + counts[1]), C_MID
    )
    norm_coef_back(R.c_o1, total, ((0, 1), (3, 4)), C_OUT, two, first.output)
    norm_coef_back(R.c_sh, total, ((0, 2), (3, 5)), C_OUT, two, first.shortcut)
    norm_back(px2, R.g2, R.c_o1, R.o1, 0, R.mk2, two.W, R.dpo, 0, C_OUT)
    R.dq[:, :px2, :] = (
        (dot(outer(R.dpo, C_OUT), R.w_o1[...], NT) * (1.0 / 9.0)).astype(BFLOAT).reshape(NIM, px2, C_MID)
    )
    halo_q = Halo(up=(R.dq.at[:, pl.ds(0, two.W)], R.dq.at[:, pl.ds(px2, two.W)]))
    halo_q.start()
    norm_back(px2, R.g2, R.c_sh, R.csh, 0, R.mk2, two.W, R.cot, 0, C_OUT)
    if inside:
        sums[tag.s2].step()
        sums[tag.r2].step()
    halo_q.finish()

    def body(i, m):
        R.dmix[i] = dot(R.spread3[...], R.dq[i])

    over_images(body)

    def window_att():
        if inside:
            sums[tag.s2].step()
            sums[tag.r2].step()
        grad_outer(tag.o1, R.q1, C_MID, R.dpo)

    def window_norm():
        if inside:
            sums[tag.s2].step()
            sums[tag.r2].step()
        grad_outer(tag.sh, R.t1, C_IN, R.cot)
        if inside:
            sums[tag.mid].step()

    def window_split():
        if inside:
            emit_squeezes()
            small_one.start()
            sums[tag.mid].step()
        R.dt1[...] = dot(outer(R.cot, C_OUT), R.w_sh[...], NT).astype(BFLOAT).reshape(NIM, px2, C_IN)
        if inside:
            sums[tag.r2].step()
            deliver(tag.o2)
            deliver(tag.s2)
            R.d_e2[...] = small_two.finish()

    def window_reduce():
        if inside:
            sums[tag.mid].step()
            sums[tag.s1].step()
            deliver(tag.r2)

    halo_d = Halo(
        (R.dp2.at[:, pl.ds(px1, edge_rows)], R.dp2.at[:, pl.ds(0, edge_rows)]),
        (R.dp2.at[:, pl.ds(edge_rows, edge_rows)], R.dp2.at[:, pl.ds(one.hp - edge_rows, edge_rows)]),
    )
    splat_back(one, halo_d, window_att, window_norm, window_split, window_reduce)

    for at in range(0, C_MID, 128):

        def body(i, m):
            term = dot(R.xh[i, edge_rows : edge_rows + px1, :], R.dp1[i, :, at : at + 128], TN)
            R.grad[:C_IN, :128] = jnp.where(i == 0, 0.0, R.grad[:C_IN, :128]) + term

        over_images(body)
        emit(tag.r1, at, R.grad[:C_IN, :128])
    if inside:
        sums[tag.r1].step()
        sums[tag.s1].step()
        sums[tag.mid].step()

    halo_d.sent()
    store_images = new_sem()
    own = pl.ds(edge_rows, px1)

    def body(i, m):
        value = dot(R.dp1[i], R.w_r1[...], NT) + dot(R.spread2[...], R.dt1[i])
        R.dp2[i, own, :] = value.astype(BFLOAT)
        pltpu.make_async_copy(R.dp2.at[i, own], R.grad_images.at[i], store_images).start()

    over_images(body)
    late.append(lambda: wait_for(R.dp2.at[:, own], store_images))
    if inside:
        sums[tag.r1].step()
        sums[tag.s1].step()
        sums[tag.mid].step()
        sums[tag.r1].step()
        for name in (tag.o1, tag.sh):
            deliver(name)
        sums[tag.s1].step()
        sums[tag.r1].step()
        sums[tag.s1].step()
        deliver(tag.s1)
        R.d_s1[...] = R.d_s1[...] + mean_term()
        total = small_one.finish()
        R.d_q1[...] = total[:8]
        R.d_q2[...] = total[8:16]
        R.d_e1[...] = total[16:]
        sums[tag.r1].step()
        deliver(tag.r1)
        for group in sums.values():
            assert group.phase == 4
    index = d * nh + h
    for full, target, length in (
        (R.all_gains, R.d_gains, GAIN_LEN // (nd * nh)),
        (R.all_shifts, R.d_shifts, SHIFT_LEN // (nd * nh)),
    ):
        start = index * length
        lane = start & (LANES - 1)
        turned = pltpu.roll(full[pl.ds(start >> 7, 8), :], lax.rem(LANES - lane, LANES), 1)
        here = iota((2, LANES), 1) < LANES - lane
        target[...] = jnp.where(here, turned[0:2], turned[1:3])
    for wait in late:
        wait()


def per_device(nd, nh, images, size_group, cotangent, *params):
    weights, (norm_gains, norm_shifts) = params[:11], params[11:]
    devices = nd * nh
    rows = images.shape[1]
    px1 = rows * H
    px2 = px1 // 4
    hp1, hp2 = px1 + 2 * H, px2 + H
    per_rows = {name: weight.shape[0] // LANES for name, weight in zip(SHAPES, weights)}
    inside = (
        nh == 4
        and devices == 32
        and per_rows[tag.q1] == 8
        and all(inner % devices == 0 for inner, _ in SHAPES.values())
    )
    axes = (tag.dp, tag.height)
    index = lax.axis_index(axes)
    cfg = types.SimpleNamespace(nd=nd, nh=nh, inside=inside, rows=rows)

    operands, names, specs = [], [], []
    whole = pl.BlockSpec(memory_space=pltpu.VMEM)

    def operand(name, value, spec=whole):
        operands.append(value)
        names.append(name)
        specs.append(spec)

    operand(tag.groups, size_group, pl.BlockSpec(memory_space=pltpu.SMEM))
    operand(tag.images, images.reshape(NIM, px1, C_IN), pl.BlockSpec(memory_space=pl.ANY))
    operand(tag.cotangent, cotangent.reshape(NIM, px2, C_OUT), pl.BlockSpec(memory_space=pl.ANY))
    if inside:
        pieces = []
        for vector in (norm_gains, norm_shifts):
            lane = lax.rem(index * vector.shape[0], LANES)
            piece = lax.dynamic_update_slice(jnp.zeros((3 * LANES,), BFLOAT), vector, (lane,))
            pieces.append(piece.reshape(3, LANES))
        operand(tag.gs, jnp.pad(jnp.concatenate(pieces, axis=0), ((0, 10), (0, 0))))
        for name, weight in zip(SHAPES, weights):
            operand(tag.a_ + name, weight.reshape(-1, LANES))
        cfg.table, total_rows = row_table(per_rows)
    else:
        for name, weight in zip(SHAPES, weights):
            full = lax.all_gather(weight, axes, axis=0, tiled=True).reshape(SHAPES[name])
            operand(tag.w_ + name, full.astype(FLOAT) if name[0] in "qe" else full)
        for name, vector, length in (
            (tag.gains, norm_gains, GAIN_ROWS),
            (tag.shifts, norm_shifts, SHIFT_ROWS),
        ):
            full = lax.all_gather(vector, axes, axis=0, tiled=True).astype(FLOAT)
            full = jnp.pad(full, (0, length * LANES - full.shape[0]))
            operand(name, full.reshape(length, LANES))

    outs = dict(
        layer_one=((NIM, px2, C_OUT), BFLOAT),
        layer_two=((NIM, px2, C_OUT), BFLOAT),
        grad_images=((NIM, px1, C_IN), BFLOAT),
    )
    for name, shape in SHAPES.items():
        outs["d_" + name] = ((per_rows[name], LANES) if inside else shape, FLOAT)
    outs[tag.d_gains] = ((2, LANES), FLOAT)
    outs[tag.d_shifts] = ((2, LANES), FLOAT)

    scratch = dict(
        xh=((NIM, hp1, C_IN), BFLOAT),
        cot=((NIM, px2, C_OUT), BFLOAT),
        mk1=((NIM, hp1, LANES), FLOAT),
        mk2=((NIM, hp2, LANES), FLOAT),
        edge1=((2, hp1, LANES), FLOAT),
        edge2=((2, MB * px2, LANES), FLOAT),
        counts=((8, LANES), FLOAT),
        all_gains=((GAIN_ROWS, LANES), FLOAT),
        all_shifts=((SHIFT_ROWS, LANES), FLOAT),
        a_sum=((8, C_MID), FLOAT),
        centre=((8, C_MID), FLOAT),
        grad_sum=((8, 2 * C_MID), FLOAT),
        acc=((MICRO, 3, 8, C_OUT), FLOAT),
        image_sums=((NIM, 8, 2 * C_MID), FLOAT),
        p1=((NIM, hp1, C_MID), FLOAT),
        a3=((NIM, hp1, 3 * C_MID), BFLOAT),
        p2=((NIM, px1, 2 * C_MID), FLOAT),
        s=((NIM, px1, 2 * C_MID), FLOAT),
        v1=((NIM, px1 + H, C_MID), BFLOAT),
        q1=((NIM, px2, C_MID), BFLOAT),
        t1=((NIM, px2, C_IN), BFLOAT),
        o1=((NIM, px2, C_OUT), FLOAT),
        csh=((NIM, px2, C_OUT), FLOAT),
        p1b=((NIM, hp2, C_MID), FLOAT),
        a3b=((NIM, hp2, 3 * C_MID), BFLOAT),
        p2b=((NIM, px2, 2 * C_MID), FLOAT),
        sb=((NIM, px2, 2 * C_MID), FLOAT),
        mix2=((NIM, px2, C_MID), BFLOAT),
        l1=((NIM, px2, C_OUT), BFLOAT),
        o2=((NIM, px2, C_OUT), FLOAT),
        g2=((NIM, px2, C_OUT), FLOAT),
        dpo=((NIM, px2, C_OUT), BFLOAT),
        dmixb=((NIM, px2, C_MID), FLOAT),
        dp2b=((NIM, hp2, 2 * C_MID), BFLOAT),
        dp1b=((NIM, px2, C_MID), BFLOAT),
        dq=((NIM, px2 + H // 2, C_MID), BFLOAT),
        dt1=((NIM, px2, C_IN), BFLOAT),
        dmix=((NIM, px1, C_MID), FLOAT),
        dp2=((NIM, hp1, 2 * C_MID), BFLOAT),
        dp1=((NIM, px1, C_MID), BFLOAT),
        grad=((9 * C_MID, C_MID), FLOAT),
        pool3=((px2, px1 + H), BFLOAT),
        pool2=((px2, px1), BFLOAT),
        spread2=((px1, px2), BFLOAT),
        spread3=((px1, px2 + H // 2), BFLOAT),
        keep1=((6, 8, 2 * C_MID), FLOAT),
        keep2=((6, 8, 2 * C_MID), FLOAT),
        att1=((NIM, 8, 2 * C_MID), FLOAT),
        att2=((NIM, 8, 2 * C_MID), FLOAT),
        dgap1=((NIM, 8, C_MID), FLOAT),
        dgap2=((NIM, 8, C_MID), FLOAT),
        c_n1=((MICRO, 8, C_MID), FLOAT),
        c_n2=((MICRO, 8, 2 * C_MID), FLOAT),
        c_o1=((MICRO, 8, C_OUT), FLOAT),
        c_sh=((MICRO, 8, C_OUT), FLOAT),
        c_n1b=((MICRO, 8, C_MID), FLOAT),
        c_n2b=((MICRO, 8, 2 * C_MID), FLOAT),
        c_o2=((MICRO, 8, C_OUT), FLOAT),
    )
    for name, (count, lanes, kind) in SYNCS.items():
        for k, size in enumerate(stage_sizes(kind, nd, nh)):
            scratch["sy_" + name + str(k)] = ((size, count, lanes), FLOAT)
    if inside:
        four = (nd // 2, 2, nh // 2, 2)
        scratch |= dict(
            pack=(four + (total_rows, LANES), BFLOAT),
            rc=(four[:3] + (total_rows, LANES), BFLOAT),
            ry=(four[:2] + (total_rows, LANES), BFLOAT),
            rx=(four[:1] + (total_rows, LANES), BFLOAT),
            rz=(four[:1] + (total_rows, LANES), BFLOAT),
            small=((nd, nh, 48, LANES), FLOAT),
            small_in=((nd, 48, LANES), FLOAT),
            gains=((GAIN_ROWS, LANES), FLOAT),
            shifts=((SHIFT_ROWS, LANES), FLOAT),
            g_q1=((C_MID, C_ATT), FLOAT),
            g_q2=((C_MID, C_ATT), FLOAT),
        )
        for name, shape in SHAPES.items():
            scratch["w_" + name] = (shape, FLOAT if name[0] in "qe" else BFLOAT)

    results = pl.pallas_call(
        functools.partial(
            kernel, cfg, names + list(outs) + list(scratch) + [tag.sem]
        ),
        out_shape=[jax.ShapeDtypeStruct(shape, kind) for shape, kind in outs.values()],
        in_specs=specs,
        out_specs=[pl.BlockSpec(memory_space=pl.ANY)] * 3 + [whole] * (len(outs) - 3),
        scratch_shapes=[pltpu.VMEM(shape, kind) for shape, kind in scratch.values()]
        + [pltpu.SemaphoreType.DMA((SEMAPHORES,))],
        compiler_params=pltpu.CompilerParams(
            collective_id=0, has_side_effects=True, vmem_limit_bytes=62 * 1024 * 1024
        ),
    )(*operands)

    if inside:
        results = deliver_all(results)
    layer_one, layer_two, grad_images = results[:3]
    grads = [grad.reshape(-1) for grad in results[3:14]]
    if not inside:
        grads = [
            lax.psum_scatter(grad, axes, scatter_dimension=0, tiled=True) for grad in grads
        ]
    tails = [
        total.reshape(-1)[: vector.shape[0]] for total, vector in zip(results[14:], (norm_gains, norm_shifts))
    ]
    return (
        layer_one.reshape(cotangent.shape),
        layer_two.reshape(cotangent.shape),
        grad_images.reshape(images.shape),
        *grads,
        *tails,
    )


def copy_all(count, *refs):
    copies = [
        pltpu.make_async_copy(source, target, refs[-1].at[k])
        for k, (source, target) in enumerate(zip(refs[:count], refs[count : 2 * count]))
    ]
    for copy in copies:
        copy.start()
    for copy in copies:
        copy.wait()


def deliver_all(results):
    count = len(results)
    anywhere = pl.BlockSpec(memory_space=pl.ANY)
    return pl.pallas_call(
        functools.partial(copy_all, count),
        out_shape=[jax.ShapeDtypeStruct(value.shape, value.dtype) for value in results],
        in_specs=[pl.BlockSpec(memory_space=pltpu.VMEM)] * count,
        out_specs=[anywhere] * count,
        scratch_shapes=[pltpu.SemaphoreType.DMA((count,))],
    )(*results)


def solution(mesh):
    shard = P(("dp", "height"))
    rows = P("dp", "height", None, None)
    return jax.shard_map(
        functools.partial(per_device, mesh.shape["dp"], mesh.shape["height"]),
        mesh=mesh,
        in_specs=(rows, P("dp"), rows) + (shard,) * 13,
        out_specs=(rows,) * 3 + (shard,) * 13,
        check_vma=False,
    )
```

profile of v0, /device:TPU:0, one launch (start us, length us, event | category | flops | bytes accessed | tf_op | source)
XLA Modules:
  0.0 235.8 jit_solution(6377878468891481337)
XLA Ops:
  0.7 0.9 dynamic_update_slice.7
  1.5 0.8 dynamic_update_slice.6
  2.4 0.6 fusion.2.refs_3_
  3.0 228.7 %shard_map.279 = (bf16[6,64,1024]{2,1,0:T(8,128)(2,1)}, bf16[6,64,1024]{2,1,0:T(8,128)(2,1)}, bf16[6,256,512]{2,1,0:T(8,128)(2,1)}, f32[32,128]{1,0:T(8,128)}, f...) custom-call(s32[6]{0:T(128)} %refs_0_.1, ...), custom_call_target="tpu_custom_call" | custom-call | tf_op jit(solution)/shard_map/pallas_call | solution.py:1648
  231.7 3.9 %shard_map.280 = (bf16[6,64,1024]{2,1,0:T(8,128)(2,1)}, bf16[6,64,1024]{2,1,0:T(8,128)(2,1)}, bf16[6,256,512]{2,1,0:T(8,128)(2,1)}, f32[32,128]{1,0:T(8,128)}, f...) custom-call(bf16[6,64,1024]{2,1,0:T(8,128)(2,1)} %get-tuple-element., ...), custom_call_target="tpu_custom_call" | custom-call | tf_op jit(solution)/shard_map/pallas_call | solution.py:1696
  (2 shorter events, 0.0 us)
where the time goes:
time: 236 us
  Pallas kernels  233 us (99%)
    pallas_call x1, Pallas kernels, per_device(): pl.pallas_call(functools.partial(kernel, cfg, names + list(outs) + list(s...  229 us

commit v1 on v0

v1 whole, which is shorter than its diff:
```python
import functools
import types

import jax
import jax.numpy as jnp
from jax import lax
from jax.experimental import pallas as pl
from jax.experimental.pallas import tpu as pltpu
from jax.sharding import PartitionSpec as P

C_IN = 512
C_MID = 256
C_ATT = 128
C_OUT = 1024
H = 32
STEP = 4
MICRO = 2
MB = 3

EPSILON = 1e-05
HIGHEST = lax.Precision.HIGHEST
FLOAT = jnp.float32
BFLOAT = jnp.bfloat16
MESH = pl.DeviceIdType.MESH
LANES = 128
NIM = MICRO * MB
NN = (((1,), (0,)), ((), ()))
NT = (((1,), (1,)), ((), ()))
TN = (((0,), (0,)), ((), ()))


class Names:
    def __getattr__(self, name):
        return name


tag = Names()

SHAPES = dict(
    r1=(C_IN, C_MID),
    s1=(9 * C_MID, C_MID),
    q1=(C_MID, C_ATT),
    e1=(C_ATT, 2 * C_MID),
    o1=(C_MID, C_OUT),
    sh=(C_IN, C_OUT),
    r2=(C_OUT, C_MID),
    s2=(9 * C_MID, C_MID),
    q2=(C_MID, C_ATT),
    e2=(C_ATT, 2 * C_MID),
    o2=(C_MID, C_OUT),
)

HEIGHT, DP, ONCE, TWICE = range(4)
SYNCS = dict(
    n1=(8, LANES, ONCE),
    n2=(8, LANES, ONCE),
    gap=(8, LANES, HEIGHT),
    na=(8, LANES, DP),
    no=(8, 4 * LANES, TWICE),
    n1b=(8, LANES, ONCE),
    n2b=(8, LANES, ONCE),
    gapb=(8, LANES, HEIGHT),
    nab=(8, LANES, DP),
    nob=(8, 2 * LANES, TWICE),
    dnob=(8, 2 * LANES, TWICE),
    dattb=(8, 2 * LANES, HEIGHT),
    dnab=(8, LANES, DP),
    dn2b=(8, LANES, ONCE),
    dn1b=(8, LANES, ONCE),
    dno=(8, 3 * LANES, TWICE),
    datt=(8, 2 * LANES, HEIGHT),
    dna=(8, LANES, DP),
    dn2=(8, LANES, ONCE),
    dn1=(8, LANES, ONCE),
)
SEMAPHORES = 384
SMALL = dict(e2=0, q=16, e1=32)


def offsets():
    first = types.SimpleNamespace(
        reduce=0,
        split=C_MID,
        attend=3 * C_MID,
        output=3 * C_MID + C_ATT,
        shortcut=3 * C_MID + C_ATT + C_OUT,
    )
    base = 3 * C_MID + C_ATT + 2 * C_OUT
    second = types.SimpleNamespace(
        reduce=base,
        split=base + C_MID,
        attend=base + 3 * C_MID,
        output=base + 3 * C_MID + C_ATT,
    )
    total = base + 3 * C_MID + C_ATT + C_OUT
    first.bias = total
    second.bias = total + 2 * C_MID
    return (first, second)


GAIN_LEN = 6 * C_MID + 2 * C_ATT + 3 * C_OUT
SHIFT_LEN = GAIN_LEN + 4 * C_MID
GAIN_ROWS = 48
SHIFT_ROWS = 56


def stage_sizes(kind, nd, nh):
    deep = nd // 2
    deep = (deep,) if deep <= 8 else (8, deep // 8)
    if kind == HEIGHT:
        return (nh,)
    if kind == DP:
        return (nd,) if nd <= 8 else deep + (2,)
    return (nd * nh,) if kind == ONCE and nd * nh <= 32 else (2 * nh,) + deep


def row_table(per_device):
    table = {}
    at = 0
    parts = dict(
        s1=per_device[tag.s1],
        o1=per_device[tag.o1],
        sh=per_device[tag.sh],
        r2=per_device[tag.r2],
        s2=per_device[tag.s2],
        o2=per_device[tag.o2],
        r1=per_device[tag.r1],
        gs=16,
        q=per_device[tag.q1] + per_device[tag.q2],
        e1=per_device[tag.e1],
        e2=per_device[tag.e2],
    )
    for name, count in parts.items():
        table[name] = (at, count)
        at += count
    return table, at


def dot(left, right, dims=NN):
    return lax.dot_general(left, right, dims, preferred_element_type=FLOAT)


def exact(left, right, dims=NN):
    return lax.dot_general(left, right, dims, preferred_element_type=FLOAT, precision=HIGHEST)


def sigmoid(values):
    return 0.5 * jnp.tanh(0.5 * values) + 0.5


def slope_of(values):
    logistic = sigmoid(values)
    return logistic * (1.0 + values * (1.0 - logistic))


def widen(part, columns):
    return jnp.concatenate([part] * (columns // LANES), axis=1)


def fold(values):
    rows, columns = values.shape
    return jnp.sum(values.reshape(rows // 8, 8, columns), axis=0)


def iota(shape, axis):
    return lax.broadcasted_iota(jnp.int32, shape, axis)


def ones_where(condition, kind=BFLOAT):
    return jnp.where(condition, 1.0, 0.0).astype(FLOAT).astype(kind)


def shuffle(count, rows, blocks, back=False):
    new = iota((count, count), 1 if back else 0)
    old = iota((count, count), 0 if back else 1)
    hit = None
    for block in range(blocks):
        same = old == blocks * new - blocks * block * rows + block
        hit = same if hit is None else hit | same
    return hit


def kernel(cfg, names, *refs):
    R = types.SimpleNamespace(**dict(zip(names, refs)))
    nd, nh, inside = cfg.nd, cfg.nh, cfg.inside
    d, h = lax.axis_index(tag.dp), lax.axis_index(tag.height)
    first, second = offsets()
    used = [0]
    late = []
    share = 1.0 if inside else 1.0 / nh

    def new_sem():
        used[0] += 1
        assert used[0] <= SEMAPHORES
        return R.sem.at[used[0] - 1]

    def remote(source, target, send, receive, device):
        return pltpu.make_async_remote_copy(
            src_ref=source,
            dst_ref=target,
            send_sem=send,
            recv_sem=receive,
            device_id=device,
            device_id_type=MESH,
        )

    def wait_for(ref, sem):
        pltpu.make_async_copy(ref, ref, sem).wait()

    x, z = lax.rem(d, 2), lax.div(d, 2)
    plane = (2 * nh, 2 * h + x, lambda q: (2 * z + lax.rem(q, 2), lax.div(q, 2)))
    if nd <= 16:
        depth = [(nd // 2, z, lambda q: (2 * q + x, h))]
    else:
        high = nd // 16
        z_low, z_high = lax.div(z, high), lax.rem(z, high)
        depth = [
            (8, z_low, lambda q: (2 * (q * high + z_high) + x, h)),
            (high, z_high, lambda q: (2 * (z_low * high + q) + x, h)),
        ]
    along_dp = [(nd, d, lambda q: (q, h))] if nd <= 8 else depth + [(2, x, lambda q: (2 * z + q, h))]
    along_height = (nh, h, lambda q: (d, q))
    every = (nd * nh, d * nh + h, lambda q: (lax.div(q, nh), lax.rem(q, nh)))
    small_mesh = nd * nh <= 32
    stages_of = {
        HEIGHT: [along_height],
        DP: along_dp,
        ONCE: [every] if small_mesh else [plane] + depth,
        TWICE: [plane] + depth,
    }

    class Exchange:
        def __init__(self, name, m):
            self.stages = stages_of[SYNCS[name][2]]
            self.bufs = [
                getattr(R, "sy_" + name + str(m) + str(k)) for k in range(len(self.stages))
            ]

        def put(self, vectors, at=0, fill=True):
            slot = self.bufs[0].at[self.stages[0][1]]
            rows, lanes = slot.shape
            for vector in vectors:
                for k in range(vector.shape[1] // LANES):
                    column = at // rows * LANES
                    slot[at % rows : at % rows + 1, column : column + LANES] = vector[
                        :, k * LANES : (k + 1) * LANES
                    ]
                    at += 1
            while fill and at < rows * lanes // LANES:
                column = at // rows * LANES
                stop = min(rows, at % rows + rows * lanes // LANES - at)
                slot[at % rows : stop, column : column + LANES] = jnp.zeros(
                    (stop - at % rows, LANES), FLOAT
                )
                at += stop - at % rows

        def send(self, stage):
            count, me, peer = self.stages[stage]
            buf = self.bufs[stage]
            send, self.receive = new_sem(), new_sem()
            for step in range(1, count):
                to = lax.rem(me + step, count)
                remote(buf.at[me], buf.at[me], send, self.receive, peer(to)).start()
            late.append(lambda: wait_for(buf.at[pl.ds(0, count - 1)], send))

        def start(self, vectors):
            self.put(vectors)
            self.send(0)

        def finish(self):
            for stage, (count, me, _) in enumerate(self.stages):
                buf = self.bufs[stage]
                if stage > 0:
                    buf[me] = total
                    self.send(stage)
                yield
                wait_for(buf.at[pl.ds(0, count - 1)], self.receive)
                total = jnp.sum(buf[...], axis=0)
            return total

    def take(total, at, length):
        rows = total.shape[0]
        parts = []
        for k in range(at, at + length // LANES):
            column = k // rows * LANES
            parts.append(total[k % rows : k % rows + 1, column : column + LANES])
        return jnp.concatenate(parts, axis=1)

    if inside:
        Z, X, Y, C = nd // 2, 2, nh // 2, 2
        y, c = lax.div(h, 2), lax.rem(h, 2)
        table = cfg.table
        G = R.pack

        def in_plane(step):
            to = lax.rem(x * Y + y + step, X * Y)
            return lax.div(to, Y), lax.rem(to, Y)

        class Gather:
            def __init__(self, start, stop, direct=False):
                self.rows = pl.ds(start, stop - start)
                self.direct = direct
                self.phase = -1
                self.sends = []
                self.waits = []

            def send(self, part, to):
                send, receive = new_sem(), new_sem()
                remote(part, part, send, receive, to).start()
                self.sends.append(lambda: wait_for(part, send))
                self.waits.append(lambda: wait_for(part, receive))

            def step(self):
                for wait in self.waits:
                    wait()
                self.waits = []
                self.phase += 1
                if self.phase == 0:
                    own = G.at[z, x, y, c, self.rows]
                    if self.direct:
                        count = Z * X * Y
                        for step in range(1, count):
                            to = lax.rem(d * Y + y + step, count)
                            self.send(own, (lax.div(to, Y), lax.rem(to, Y) * 2 + c))
                        self.phase = 1
                    else:
                        for step in range(1, Z):
                            self.send(own, (lax.rem(z + step, Z) * 2 + x, h))
                elif self.phase == 1:
                    for step in range(1, X * Y):
                        xx, yy = in_plane(step)
                        self.send(G.at[:, x, y, c, self.rows], (z * 2 + xx, yy * 2 + c))
                elif self.phase == 2:
                    self.send(G.at[:, :, :, c, self.rows], (d, y * 2 + 1 - c))

            def finish(self):
                while self.phase < 3:
                    self.step()

            def sent(self):
                for wait in self.sends:
                    wait()

        class Scatter:
            def __init__(self, start, stop):
                self.rows = pl.ds(start, stop - start)
                self.phase = -1
                self.waits = []

            def begin(self, source, target, to):
                send, receive = new_sem(), new_sem()
                remote(source, target, send, receive, to).start()
                late.append(lambda: wait_for(source, send))
                self.waits.append(lambda: wait_for(target, receive))

            def step(self):
                rows = self.rows
                for wait in self.waits:
                    wait()
                self.waits = []
                self.phase += 1
                if self.phase == 0:
                    self.begin(G.at[:, :, :, 1 - c, rows], R.rc.at[:, :, :, rows], (d, y * 2 + 1 - c))
                elif self.phase == 1:

                    def add(zz, _):
                        for xx in range(X):
                            for yy in range(Y):
                                mine = G[zz, xx, yy, c, rows].astype(FLOAT)
                                G[zz, xx, yy, c, rows] = (
                                    mine + R.rc[zz, xx, yy, rows].astype(FLOAT)
                                ).astype(BFLOAT)
                        return 0

                    lax.fori_loop(0, Z, add, 0)
                    for step in range(1, X * Y):
                        xx, yy = in_plane(step)
                        self.begin(
                            G.at[:, xx, yy, c, rows],
                            R.rp.at[step - 1, :, rows],
                            (z * 2 + xx, yy * 2 + c),
                        )
                elif self.phase == 2:

                    def add(zz, _):
                        total = G[zz, x, y, c, rows].astype(FLOAT)
                        for k in range(X * Y - 1):
                            total = total + R.rp[k, zz, rows].astype(FLOAT)
                        G[zz, x, y, c, rows] = total.astype(BFLOAT)
                        return 0

                    lax.fori_loop(0, Z, add, 0)
                    for step in range(1, Z):
                        to = lax.rem(z + step, Z)
                        self.begin(
                            G.at[to, x, y, c, rows], R.rz.at[step - 1, rows], (to * 2 + x, h)
                        )

            def finish(self):
                while self.phase < 3:
                    self.step()

        def scattered(name):
            start, count = table[name]
            rows = pl.ds(start, count)
            total = G[z, x, y, c, rows].astype(FLOAT)
            for k in range(Z - 1):
                total = total + R.rz[k, rows].astype(FLOAT)
            return total

        def own_rows(name, values):
            start, count = table[name]
            G[z, x, y, c, start : start + count] = values.astype(BFLOAT)

        def per_dev(name):
            return SHAPES[name][0] // (nd * nh)

        def pack_shards(*parts):
            for name in parts:
                rows, blocks = per_dev(name), SHAPES[name][1] // LANES
                order = ones_where(shuffle(rows * blocks, rows, blocks))
                own_rows(name, dot(order, getattr(R, "a_" + name)[...]))

        def pack_small():
            own_rows(
                "q", jnp.concatenate([R.a_q1[...].astype(FLOAT), R.a_q2[...].astype(FLOAT)], axis=0)
            )
            own_rows(tag.e1, R.a_e1[...])
            own_rows(tag.e2, R.a_e2[...])

        def unpack_rows(name):
            rows, blocks = per_dev(name), SHAPES[name][1] // LANES
            start = table[name][0]
            full = getattr(R, "w_" + name)
            for block in range(blocks):
                at = start + block * rows
                full[:, block * LANES : (block + 1) * LANES] = G[
                    :, :, :, :, at : at + rows, :
                ].reshape(nd * nh * rows, LANES)

        def unpack_pairs(name):
            blocks = SHAPES[name][1] // LANES
            start = table[name][0]
            full = getattr(R, "w_" + name)
            for pair in range(blocks // 2):
                at = start + 16 * pair
                both = G[:, :, :, :, at : at + 16, :].astype(FLOAT).reshape(nd * nh, 2, 8, LANES)
                for one in range(2):
                    block = 2 * pair + one
                    full[:, block * LANES : (block + 1) * LANES] = (
                        both[:, one].reshape(nd * nh * 8, LANES).astype(BFLOAT)
                    )

        def unpack_split(name):
            start, count = table[name]
            full = getattr(R, "w_" + name)
            rows = per_dev(name)
            group = nh * rows

            def body(j, _):
                zz, xx = lax.div(j, 2), lax.rem(j, 2)
                part = G[zz, xx, :, :, start : start + count, :].astype(FLOAT)
                part = part.reshape(nh, 2, rows, LANES)
                at = pl.ds(pl.multiple_of(j * group, group), group)
                for block in range(2):
                    full[at, block * LANES : (block + 1) * LANES] = (
                        part[:, block].reshape(group, LANES).astype(BFLOAT)
                    )
                return 0

            lax.fori_loop(0, nd, body, 0)

        def unpack_attention():
            at = table[tag.q][0]
            both = G[:, :, :, :, at : at + 16, :].astype(FLOAT).reshape(nd * nh, 2, 8, LANES)
            R.w_q1[...] = both[:, 0].reshape(C_MID, C_ATT)
            R.w_q2[...] = both[:, 1].reshape(C_MID, C_ATT)
            for name in (tag.e1, tag.e2):
                at = table[name][0]
                part = G[:, :, :, :, at : at + 16, :].reshape(4 * C_ATT, LANES)
                for block in range(4):
                    pick = ones_where(
                        iota((C_ATT, 4 * C_ATT), 1) == 4 * iota((C_ATT, 4 * C_ATT), 0) + block
                    )
                    getattr(R, "w_" + name)[:, block * LANES : (block + 1) * LANES] = dot(pick, part)

        def unpack_gains():
            at = table[tag.gs][0]
            part = G[:, :, :, :, at : at + 16, :].reshape(16 * nd * nh, LANES)
            for full, rows, first_row, length in (
                (R.gains, GAIN_ROWS, 0, GAIN_LEN // (nd * nh)),
                (R.shifts, SHIFT_ROWS, 3, SHIFT_LEN // (nd * nh)),
            ):
                shape = (rows, 16 * nd * nh)
                source = iota(shape, 1)
                row = (source & 15) - first_row
                target = (((source >> 4) * length) >> 7) + row
                hit = (row >= 0) & (row < 3) & (target == iota(shape, 0))
                full[...] = dot(ones_where(hit), part)

        def emit(name, at, values):
            start = table[name][0] if name[0] != "q" else 0
            rows = per_dev(name)
            if rows % 16 == 0:
                for block in range(values.shape[1] // LANES):
                    to = start + (at // LANES + block) * rows
                    part = values[:, block * LANES : (block + 1) * LANES].astype(BFLOAT)
                    G[:, :, :, :, to : to + rows, :] = part.reshape(Z, X, Y, C, rows, LANES)
            elif name[0] == "o":
                for pair in range(values.shape[1] // (2 * LANES)):
                    to = start + (at // LANES + 2 * pair) * 8
                    both = [
                        values[:, (2 * pair + one) * LANES : (2 * pair + one + 1) * LANES].reshape(
                            nd * nh, 8, LANES
                        )
                        for one in range(2)
                    ]
                    part = jnp.concatenate(both, axis=1).astype(BFLOAT)
                    G[:, :, :, :, to : to + 16, :] = part.reshape(Z, X, Y, C, 16, LANES)
            elif name[0] == "e":
                part = None
                for block in range(4):
                    place = ones_where(
                        iota((4 * C_ATT, C_ATT), 0) == 4 * iota((4 * C_ATT, C_ATT), 1) + block, FLOAT
                    )
                    term = exact(place, values[:, block * LANES : (block + 1) * LANES])
                    part = term if part is None else part + term
                at = SMALL[name]
                R.small[:, :, at : at + 16, :] = part.reshape(nd, nh, 16, LANES)
            elif name[0] == "q":
                getattr(R, "g_" + name)[...] = values

        def emit_squeezes():
            both = [part[...].reshape(nd * nh, 8, LANES) for part in (R.g_q1, R.g_q2)]
            part = jnp.concatenate(both, axis=1)
            at = SMALL[tag.q]
            R.small[:, :, at : at + 16, :] = part.reshape(nd, nh, 16, LANES)

        class SmallScatter:
            def __init__(self, start, count):
                self.rows = pl.ds(start, count)

            def start(self):
                send, self.receive = new_sem(), new_sem()
                rows = self.rows
                for step in range(1, nd):
                    to = lax.rem(d + step, nd)
                    source, target = R.small.at[to, h, rows], R.small_in.at[d, rows]
                    remote(source, target, send, self.receive, (to, h)).start()
                late.append(lambda: wait_for(R.small_in.at[pl.ds(0, nd - 1), rows], send))

            def finish(self):
                wait_for(R.small_in.at[pl.ds(0, nd - 1), self.rows], self.receive)
                total = R.small[d, h, self.rows]
                for step in range(1, nd):
                    total = total + R.small_in[lax.rem(d + step, nd), self.rows]
                return total

        def emit_split(name, g):
            start, count = table[name]
            rows = per_dev(name)
            group = nh * rows

            def body(j, _):
                zz, xx = lax.div(j, 2) + g * (Z // 2), lax.rem(j, 2)
                at = pl.ds(pl.multiple_of(j * group, group), group)
                both = [
                    R.grad[at, block * LANES : (block + 1) * LANES].reshape(nh, rows, LANES)
                    for block in range(2)
                ]
                part = jnp.concatenate(both, axis=1).astype(BFLOAT)
                G[zz, xx, :, :, start : start + count, :] = part.reshape(Y, C, count, LANES)
                return 0

            lax.fori_loop(0, nd // 2, body, 0)

        def deliver(name):
            rows, blocks = per_dev(name), SHAPES[name][1] // LANES
            order = ones_where(shuffle(rows * blocks, rows, blocks, back=True), FLOAT)
            getattr(R, "d_" + name)[...] = exact(order, scattered(name))

        def range_of(*parts):
            return (table[parts[0]][0], table[parts[-1]][0] + table[parts[-1]][1])

        gather_first = Gather(*range_of(tag.r1, tag.gs), direct=True)
        gather_split = Gather(*range_of(tag.s1))
        gather_small = Gather(*range_of(tag.q, tag.e2), direct=True)
        gather_outer = Gather(*range_of(tag.o1, tag.sh))
        gather_last = Gather(*range_of(tag.r2, tag.o2))
        sums = dict(
            o2=Scatter(*range_of(tag.o2)),
            s2=Scatter(*range_of(tag.s2)),
            r2=Scatter(*range_of(tag.r2)),
            mid=Scatter(*range_of(tag.o1, tag.sh)),
            s1=Scatter(*range_of(tag.s1)),
            r1=Scatter(*range_of(tag.r1)),
        )
        small_two, small_one = SmallScatter(0, 16), SmallScatter(16, 32)
    else:

        def emit(name, at, values):
            getattr(R, "d_" + name)[:, at : at + values.shape[1]] = values

        def emit_split(name, g):
            half = R.grad.shape[0]
            getattr(R, "d_" + name)[g * half : (g + 1) * half, :] = R.grad[...]

    def vector(ref, at, length):
        row = at // LANES
        return jnp.concatenate([ref[row + k : row + k + 1, :] for k in range(length // LANES)], axis=1)

    def store_vector(m, ref, at, values):
        row = at // LANES
        for k in range(values.shape[1] // LANES):
            part = values[:, k * LANES : (k + 1) * LANES]
            ref[row + k : row + k + 1, :] = part if m == 0 else ref[row + k : row + k + 1, :] + part

    def over_images(m, body):
        def step(i, _):
            body(m * MB + i)
            return 0

        lax.fori_loop(0, MB, step, 0)

    one = types.SimpleNamespace(
        suffix="", W=H, px=cfg.rows * H, hp=(cfg.rows + 2) * H, place=first, mk=R.mk1, edge=R.edge1, p1=R.p1,
        a3=R.a3, p2=R.p2, s=R.s, dp2=R.dp2, dmix=R.dmix, dy1=R.dmix, dp1=R.dp1, c1=R.c_n1, c2=R.c_n2, group=1,
        split=R.w_s1, squeeze=R.w_q1, expand=R.w_e1, att=R.att1, dgap=R.dgap1, count=0, keep=R.keep1, k="1",
    )
    two = types.SimpleNamespace(
        suffix="b", W=H // 2, px=cfg.rows * H // 4, hp=(cfg.rows // 2 + 2) * H // 2, place=second, mk=R.mk2,
        edge=R.edge2, p1=R.p1b, a3=R.a3b, p2=R.p2b, s=R.sb, dp2=R.dp2b, dmix=R.dmixb, dy1=R.dmixb, dp1=R.dp1b,
        c1=R.c_n1b, c2=R.c_n2b, group=MB, split=R.w_s2, squeeze=R.w_q2, expand=R.w_e2, att=R.att2,
        dgap=R.dgap2, count=2, keep=R.keep2, k="2",
    )
    px1, px2 = one.px, two.px
    edge_rows = H

    def images_of(m):
        return pl.ds(m * MB, MB)

    def build_masks(block):
        bits = block.W.bit_length() - 1
        shape = (block.hp, LANES)
        pixel = iota(shape, 0)
        column = pixel & (block.W - 1)
        place = iota(block.edge.shape[1:], 0) & (block.W - 1)
        block.edge[0] = ones_where(place != 0, FLOAT)
        block.edge[1] = ones_where(place != block.W - 1, FLOAT)
        row = (pixel >> bits) - 1 + h * (block.px // block.W)
        for i in range(NIM):
            limit = (H - STEP * (2 - R.groups[i])) // (1 if block is one else 2)
            inside_grid = (row >= 0) & (row < limit) & (column < limit)
            block.mk[i] = ones_where(inside_grid, FLOAT)

    def clear(ref):
        ref[...] = jnp.zeros(ref.shape, ref.dtype)

    def totals(m, kinds, columns):
        return [
            jnp.sum(R.acc[m, kind, :, :columns], axis=0, keepdims=True) for kind in range(kinds)
        ]

    def clear_acc(m, kinds, columns):
        for kind in range(kinds):
            R.acc[m, kind, :, :columns] = jnp.zeros((8, columns), FLOAT)

    def chunk_of(columns):
        return 32 if columns <= 512 else 16

    def stat_pass(m, source, start, px, columns, mk, mask_start):
        chunk = chunk_of(columns)
        clear_acc(m, 2, columns)

        def body(i):
            total, square = R.acc[m, 0, :, :columns], R.acc[m, 1, :, :columns]
            for t in range(0, px, chunk):
                v = source[i, start + t : start + t + chunk, :]
                vm = v * widen(mk[i, mask_start + t : mask_start + t + chunk, :], columns)
                total = total + fold(vm)
                square = square + fold(vm * v)
            R.acc[m, 0, :, :columns] = total
            R.acc[m, 1, :, :columns] = square

        over_images(m, body)
        return totals(m, 2, columns)

    def inverse_count(block, m, columns):
        return widen(R.counts[block.count + m : block.count + m + 1, :], columns)

    def norm_coef(m, coef, total, at, columns, block, offset):
        gain, shift = vector(R.gains, offset, columns), vector(R.shifts, offset, columns)
        inverse = inverse_count(block, m, columns)
        step = columns // LANES
        centre = take(total, at, columns) * inverse
        scaled = lax.rsqrt(take(total, at + step, columns) * inverse - centre * centre + EPSILON)
        coef[m, 0:1, :] = gain * scaled
        coef[m, 1:2, :] = shift - centre * (gain * scaled)
        coef[m, 2:3, :] = scaled
        coef[m, 3:4, :] = -centre * scaled

    def norm_coef_back(m, coef, total, at_sum, at_along, columns, block, offset):
        inverse = inverse_count(block, m, columns)
        summed, along = take(total, at_sum, columns), take(total, at_along, columns)
        scale = -coef[m, 0:1, :] * inverse
        coef[m, 4:5, :] = scale * (summed + along * coef[m, 3:4, :])
        coef[m, 5:6, :] = scale * along * coef[m, 2:3, :]
        store_vector(m, R.all_shifts, offset, summed)
        store_vector(m, R.all_gains, offset, along)

    class Halo:
        def __init__(self, down=None, up=None):
            self.ways = []
            for pair, step in ((down, 1), (up, -1)):
                if pair is not None:
                    sends = h < nh - 1 if step == 1 else h > 0
                    gets = h > 0 if step == 1 else h < nh - 1
                    copy = remote(pair[0], pair[1], new_sem(), new_sem(), (d, h + step))
                    self.ways.append((sends, gets, copy))

        def start(self):
            for sends, _, copy in self.ways:
                pl.when(sends)(copy.start)
            late.append(self.sent)

        def finish(self):
            for _, gets, copy in self.ways:
                pl.when(gets)(copy.wait_recv)

        def sent(self):
            for sends, _, copy in self.ways:
                pl.when(sends)(copy.wait_send)
            self.ways = []

    def rims(m, block, ref):
        image, width = images_of(m), block.W
        return Halo(
            (ref.at[image, pl.ds(block.px, width)], ref.at[image, pl.ds(0, width)]),
            (ref.at[image, pl.ds(width, width)], ref.at[image, pl.ds(block.hp - width, width)]),
        )

    def clear_rim(block, ref):
        shape = (NIM, block.W, ref.shape[-1])

        @pl.when(h == 0)
        def _():
            ref[:, : block.W, :] = jnp.zeros(shape, ref.dtype)

        @pl.when(h == nh - 1)
        def _():
            ref[:, block.hp - block.W :, :] = jnp.zeros(shape, ref.dtype)

    def activate(m, block):
        half = C_MID // 2

        def body(i):
            mask = block.mk[i]
            for g in range(2):
                cols = slice(g * half, (g + 1) * half)
                value = block.c1[m, 0:1, cols] * block.p1[i, :, cols] + block.c1[m, 1:2, cols]
                value = value * sigmoid(value) * mask
                if block is one:
                    R.a_sum[m, :, cols] = R.a_sum[m, :, cols] + fold(
                        value[block.W : block.W + block.px]
                    )
                at = 3 * g * half
                left = pltpu.roll(value, 1, 0) * block.edge[0, : block.hp]
                right = pltpu.roll(value, block.hp - 1, 0) * block.edge[1, : block.hp]
                block.a3[i, :, at : at + half] = left.astype(BFLOAT)
                block.a3[i, :, at + half : at + 2 * half] = value.astype(BFLOAT)
                block.a3[i, :, at + 2 * half : at + 3 * half] = right.astype(BFLOAT)

        over_images(m, body)

    def rows_of(ref, i, count, start, rows, cols):
        part = ref[pl.ds(i, count), start : start + rows, cols]
        return part.reshape(count * rows, part.shape[-1])

    def convolve(m, block):
        half = C_MID // 2
        for g in range(2):
            cols = slice(3 * g * half, 3 * (g + 1) * half)
            taps = [
                rows_of(block.a3, m * MB, MB, dy * block.W, block.px, cols) for dy in range(3)
            ]
            matrix = block.split[9 * g * half : 9 * (g + 1) * half, :]
            result = dot(jnp.concatenate(taps, axis=1), matrix)
            block.p2[images_of(m), :, g * C_MID : (g + 1) * C_MID] = result.reshape(
                MB, block.px, C_MID
            )

    def split_activate(m, block):
        columns = 2 * C_MID

        def body(i):
            gap = jnp.zeros((8, C_MID), FLOAT)
            for t in range(0, block.px, 32):
                at = slice(t, t + 32)
                mask = widen(block.mk[i, block.W + t : block.W + t + 32, :], columns)
                value = block.c2[m, 0:1, :] * block.p2[i, at, :] + block.c2[m, 1:2, :]
                value = value * sigmoid(value) * mask
                block.s[i, at, :] = value
                gap = gap + fold(value[:, :C_MID] + value[:, C_MID:])
            R.image_sums[i, :, :C_MID] = gap

        over_images(m, body)

    def image_rows(m, columns):
        return [
            jnp.sum(R.image_sums[i, :, :columns], axis=0, keepdims=True)
            for i in range(m * MB, (m + 1) * MB)
        ]

    def inverse_area(block, i):
        limit = (H - STEP * (2 - R.groups[i])) // (1 if block is one else 2)
        side = jnp.full((1, C_MID), limit.astype(FLOAT))
        return 1.0 / (side * side)

    def attend(m, block, window_gap, window_norm):
        suffix = block.suffix
        gap, norm = Exchange(tag.gap + suffix, m), Exchange(tag.na + suffix, m)
        split_activate(m, block)
        gap.start(image_rows(m, C_MID))
        window_gap()
        total = yield from gap.finish()
        keep = block.keep.at[m]
        for k in range(MB):
            keep[0, k : k + 1, :C_MID] = take(total, 2 * k, C_MID) * inverse_area(block, m * MB + k)
        before = exact(keep[0, :, :C_MID], block.squeeze[...])
        norm.start(
            [
                jnp.sum(before, axis=0, keepdims=True),
                jnp.sum(before * before, axis=0, keepdims=True),
            ]
        )
        window_norm()
        total = yield from norm.finish()
        count = MB * nd
        centre = total[0:1] / count
        scaled = lax.rsqrt(total[1:2] / count - centre * centre + EPSILON)
        normal = (before - centre) * scaled
        gain = vector(R.gains, block.place.attend, C_ATT)
        shift = vector(R.shifts, block.place.attend, C_ATT)
        normed = gain * normal + shift
        hidden = normed * sigmoid(normed)
        keep[1, :, :C_ATT] = normal
        keep[2, :, :C_ATT] = normed
        keep[3, :, :C_ATT] = hidden
        keep[4, 0:1, :C_ATT] = gain * scaled
        logits = exact(hidden, block.expand[...]) + vector(R.shifts, block.place.bias, 2 * C_MID)
        gap_logit = logits[:, :C_MID] - logits[:, C_MID:]
        keep[5, :, :] = jnp.concatenate([sigmoid(gap_logit), sigmoid(-gap_logit)], axis=1)
        for k in range(MB):
            block.att[m * MB + k] = jnp.broadcast_to(keep[5, k : k + 1, :], (8, 2 * C_MID))

    def mix(m, block, target, start):
        def body(i):
            for t in range(0, block.px, 32):
                at = slice(t, t + 32)
                value = (
                    block.att[i, 0:1, :C_MID] * block.s[i, at, :C_MID]
                    + block.att[i, 0:1, C_MID:] * block.s[i, at, C_MID:]
                )
                target[i, start + t : start + t + 32, :] = value.astype(BFLOAT)

        over_images(m, body)

    def attend_back(m, block, window_att, window_norm):
        suffix = block.suffix

        def body(i):
            parts = [jnp.zeros((8, C_MID), FLOAT)] * 2
            for t in range(0, block.px, 32):
                at = slice(t, t + 32)
                grad = block.dmix[i, at, :]
                for j in range(2):
                    parts[j] = parts[j] + fold(grad * block.s[i, at, j * C_MID : (j + 1) * C_MID])
            R.image_sums[i] = jnp.concatenate(parts, axis=1)

        over_images(m, body)
        heights, norm = Exchange(tag.datt + suffix, m), Exchange(tag.dna + suffix, m)
        heights.start(image_rows(m, 2 * C_MID))
        window_att()
        total = yield from heights.finish()
        keep = block.keep.at[m]
        for k in range(MB):
            keep[6, k : k + 1, :] = take(total, 4 * k, 2 * C_MID)
        att = keep[5]
        weighted = att * keep[6]
        both = weighted[:, :C_MID] + weighted[:, C_MID:]
        grad_logits = weighted - att * jnp.concatenate([both, both], axis=1)
        keep[6] = grad_logits
        grad_hidden = exact(grad_logits, block.expand[...], NT)
        grad_normed = grad_hidden * slope_of(keep[2, :, :C_ATT])
        normal = keep[1, :, :C_ATT]
        norm.start(
            [
                jnp.sum(grad_normed, axis=0, keepdims=True),
                jnp.sum(grad_normed * normal, axis=0, keepdims=True),
                jnp.sum(grad_logits, axis=0, keepdims=True),
            ]
        )
        window_norm()
        total = yield from norm.finish()
        count = MB * nd
        store_vector(m, R.all_shifts, block.place.attend, total[0:1])
        store_vector(m, R.all_gains, block.place.attend, total[1:2])
        store_vector(m, R.all_shifts, block.place.bias, take(total, 2, 2 * C_MID))
        grad_before = keep[4, 0:1, :C_ATT] * (grad_normed - (total[0:1] + normal * total[1:2]) / count)
        keep[7, :, :C_ATT] = grad_before
        grad_gap = exact(grad_before, block.squeeze[...], NT)
        for k in range(MB):
            row = grad_gap[k : k + 1, :] * inverse_area(block, m * MB + k)
            block.dgap[m * MB + k] = jnp.broadcast_to(row, (8, C_MID))

    def small_grads(block, squeeze):
        left, right, wide = (0, 7, C_ATT) if squeeze else (3, 6, 2 * C_MID)
        tall = C_MID if squeeze else C_ATT
        total = None
        for m in range(MICRO):
            term = exact(block.keep[m, left, :, :tall], block.keep[m, right, :, :wide], TN)
            total = term if total is None else total + term
        emit((tag.q if squeeze else tag.e) + block.k, 0, total * share)

    def split_back(m, block):
        clear_acc(m, 2, 2 * C_MID)

        def body(i):
            for j in range(2):
                cols = slice(j * C_MID, (j + 1) * C_MID)
                total, along = R.acc[m, 0, :, cols], R.acc[m, 1, :, cols]
                for t in range(0, block.px, 32):
                    at = slice(t, t + 32)
                    mask = widen(block.mk[i, block.W + t : block.W + t + 32, :], C_MID)
                    raw = block.p2[i, at, cols]
                    value = block.c2[m, 0:1, cols] * raw + block.c2[m, 1:2, cols]
                    grad = block.att[i, 0:1, cols] * block.dmix[i, at, :] + block.dgap[i, 0:1, :]
                    grad = grad * slope_of(value) * mask
                    block.s[i, at, cols] = grad
                    total = total + fold(grad)
                    along = along + fold(
                        grad * (block.c2[m, 2:3, cols] * raw + block.c2[m, 3:4, cols])
                    )
                R.acc[m, 0, :, cols] = total
                R.acc[m, 1, :, cols] = along

        over_images(m, body)

    def norm_back(m, block_px, grad, coef, raw, raw_start, mk, mask_start, target, start, columns, sums_=False):
        chunk = chunk_of(columns)
        if sums_:
            R.acc[m, 2, :, :columns] = jnp.zeros((8, columns), FLOAT)

        def body(i):
            for t in range(0, block_px, chunk):
                mask = widen(mk[i, mask_start + t : mask_start + t + chunk, :], columns)
                value = (
                    coef[m, 0:1, :] * grad[i, t : t + chunk, :]
                    + coef[m, 4:5, :]
                    + coef[m, 5:6, :] * raw[i, raw_start + t : raw_start + t + chunk, :]
                )
                value = (value * mask).astype(BFLOAT)
                target[i, start + t : start + t + chunk, :] = value
                if sums_:
                    R.acc[m, 2, :, :columns] = R.acc[m, 2, :, :columns] + fold(value.astype(FLOAT))

        over_images(m, body)

    def mean_activation():
        return 0.5 * (R.centre[0:1, :] + R.centre[1:2, :])

    def product_of_means(g):
        half = C_MID // 2
        cols = slice(g * C_MID, (g + 1) * C_MID)
        eye = iota((half, half), 0) == iota((half, half), 1)
        row = jnp.broadcast_to(mean_activation()[:, g * half : (g + 1) * half], (half, half))
        column = jnp.sum(jnp.where(eye, row, 0.0), axis=1, keepdims=True)
        return column * (R.grad_sum[0:1, cols] + R.grad_sum[1:2, cols])

    def mean_term():
        half = C_MID // 2
        rows = SHAPES[tag.s1][0] // (nd * nh)
        index = d * nh + h
        low = index * rows < 9 * half
        mean = mean_activation()
        centre = jnp.where(low, mean[:, :half], mean[:, half:])
        sums_ = R.grad_sum[2:3, :] + R.grad_sum[3:4, :]
        sums_ = jnp.where(low, sums_[:, :C_MID], sums_[:, C_MID:])
        shape = (2 * rows, LANES)
        row = iota(shape, 0)
        hit = iota(shape, 1) == ((index * rows + (row >> 1)) & (half - 1))
        column = jnp.sum(
            jnp.where(hit, jnp.broadcast_to(centre, shape), 0.0), axis=1, keepdims=True
        )
        odd = (row & 1) == 1
        return column * jnp.where(
            odd, jnp.broadcast_to(sums_[:, LANES:], shape), jnp.broadcast_to(sums_[:, :LANES], shape)
        )

    def kernel_grad(block, g):
        half = C_MID // 2
        images = MB if block.group == 1 else NIM
        for dy in range(3):
            at = slice(3 * dy * half, 3 * (dy + 1) * half)
            total = None
            for i in range(0, NIM, images):
                taps = rows_of(
                    block.a3, i, images, dy * block.W, block.px, slice(3 * g * half, 3 * (g + 1) * half)
                )
                grad = rows_of(
                    block.dp2, i, images, block.W, block.px, slice(g * C_MID, (g + 1) * C_MID)
                )
                term = dot(taps, grad, TN)
                total = term if total is None else total + term
            if inside and block is one:
                total = total - jnp.concatenate([product_of_means(g)] * 3, axis=0)
            R.grad[at, :] = total

    def convolve_back(m, block):
        half = C_MID // 2
        clear_acc(m, 2, C_MID)

        def body(i, count):
            rows = count * block.px
            for g in range(2):
                cols = slice(g * half, (g + 1) * half)
                total = None
                for dy in range(3):
                    grad = rows_of(
                        block.dp2, i, count, (2 - dy) * block.W, block.px, slice(g * C_MID, (g + 1) * C_MID)
                    )
                    at = 9 * g * half + 3 * dy * half
                    term = dot(grad, block.split[at : at + 3 * half, :], NT)
                    total = term if total is None else total + term
                value = (
                    total[:, half : 2 * half]
                    + pltpu.roll(total[:, :half], rows - 1, 0) * block.edge[1, :rows]
                    + pltpu.roll(total[:, 2 * half :], 1, 0) * block.edge[0, :rows]
                )
                raw = rows_of(block.p1, i, count, block.W, block.px, cols)
                mask = rows_of(block.mk, i, count, block.W, block.px, slice(0, LANES))
                before = block.c1[m, 0:1, cols] * raw + block.c1[m, 1:2, cols]
                value = value * slope_of(before) * mask
                block.dy1[pl.ds(i, count), :, cols] = value.reshape(count, block.px, half)
                normal = block.c1[m, 2:3, cols] * raw + block.c1[m, 3:4, cols]
                R.acc[m, 0, :, cols] = R.acc[m, 0, :, cols] + fold(value)
                R.acc[m, 1, :, cols] = R.acc[m, 1, :, cols] + fold(value * normal)

        if block.group == 1:
            over_images(m, lambda i: body(i, 1))
        else:
            body(m * MB, MB)

    def splat_back(m, block, window_att, window_norm, window_split, window_halo, window_reduce):
        suffix = block.suffix
        yield from attend_back(m, block, window_att, window_norm)
        split_back(m, block)
        exchange = Exchange(tag.dn2 + suffix, m)
        exchange.start(totals(m, 2, 2 * C_MID))
        window_split()
        total = yield from exchange.finish()
        norm_coef_back(m, block.c2, total, 0, 4, 2 * C_MID, block, block.place.split)
        norm_back(
            m, block.px, block.s, block.c2, block.p2, 0, block.mk, block.W, block.dp2, block.W, 2 * C_MID,
            sums_=block is one,
        )
        block.halo[m] = rims(m, block, block.dp2)
        block.halo[m].start()
        if block is one:
            R.grad_sum[m : m + 1, :] = jnp.sum(R.acc[m, 2, :, : 2 * C_MID], axis=0, keepdims=True)
        window_halo()
        yield
        block.halo[m].finish()
        convolve_back(m, block)
        exchange = Exchange(tag.dn1 + suffix, m)
        sums_ = totals(m, 2, C_MID)
        if block is one:
            sums_.append(R.grad_sum[m : m + 1, :])
        exchange.start(sums_)
        window_reduce()
        total = yield from exchange.finish()
        if block is one:
            R.grad_sum[2 + m : 3 + m, :] = take(total, 4, 2 * C_MID)
        norm_coef_back(m, block.c1, total, 0, 2, C_MID, block, block.place.reduce)
        norm_back(
            m, block.px, block.dy1, block.c1, block.p1, block.W, block.mk, block.W, block.dp1, 0, C_MID
        )

    def nothing():
        pass

    def when_last(m, *steps):
        def window():
            if m == MICRO - 1:
                for step in steps:
                    step()

        return window

    def step_of(name):
        return sums[name].step if inside else nothing

    def hand_out(*parts):
        def step():
            if inside:
                for name in parts:
                    deliver(name)

        return step

    def outer(m, ref, columns):
        return ref[images_of(m)].reshape(MB * px2, columns)

    def product_out(m, source, inner, matrix, target):
        for at in range(0, C_OUT, 256):
            target[images_of(m), :, at : at + 256] = dot(
                outer(m, source, inner), matrix[:, at : at + 256]
            ).reshape(MB, px2, 256)

    def grad_outer(name, source, inner, grad):
        def step():
            left = source[...].reshape(NIM * px2, inner)
            for at in range(0, C_OUT, 256):
                part = grad[:, :, at : at + 256].reshape(NIM * px2, 256)
                emit(name, at, dot(left, part, TN))

        return step

    def grad_reduce_two():
        left = R.l1[...].reshape(NIM * px2, C_OUT)
        right = R.dp1b[...].reshape(NIM * px2, C_MID)
        for at in range(0, C_MID, LANES):
            emit(tag.r2, at, dot(left, right[:, at : at + LANES], TN))

    def grad_split(block):
        def step():
            for g in range(2):
                kernel_grad(block, g)
                emit_split(tag.s + block.k, g)

        return step

    def gradients_sent():
        if inside:
            for gather in (gather_first, gather_split, gather_small, gather_outer, gather_last):
                gather.sent()

    halo_x = Halo(
        (R.images.at[:, pl.ds(px1 - edge_rows, edge_rows)], R.xh.at[:, pl.ds(0, edge_rows)]),
        (R.images.at[:, pl.ds(0, edge_rows)], R.xh.at[:, pl.ds(one.hp - edge_rows, edge_rows)]),
    )
    barrier = pltpu.get_barrier_semaphore()
    partners = 0
    groups = [every] if small_mesh else [along_height, plane] + along_dp + depth
    for count, me, peer in groups:
        for step in range(1, count):
            to = peer(lax.rem(me + step, count))
            pl.semaphore_signal(barrier, inc=1, device_id=to, device_id_type=MESH)
        partners += count - 1
    load_x = pltpu.make_async_copy(R.images, R.xh.at[:, pl.ds(edge_rows, px1)], new_sem())
    load_cot = pltpu.make_async_copy(R.cotangent, R.cot, new_sem())
    load_x.start()
    load_cot.start()
    if inside:
        pack_shards(tag.r1)
        own_rows(tag.gs, R.gs[...])
    pl.semaphore_wait(barrier, partners)
    if inside:
        gather_first.step()
    halo_x.start()
    if inside:
        pack_shards(tag.s1)
        gather_split.step()
        pack_small()
    build_masks(one)

    def pool_matrices():
        out_shape = (px2, px1 + edge_rows)
        out_pixel, in_pixel = iota(out_shape, 0), iota(out_shape, 1)
        down = (in_pixel >> 5) - 2 * (out_pixel >> 4)
        along = (in_pixel & 31) - 2 * (out_pixel & 15) + 1
        R.pool3[...] = ones_where((down >= 0) & (down < 3) & (along >= 0) & (along < 3))
        out_shape = (px2, px1)
        out_pixel, in_pixel = iota(out_shape, 0), iota(out_shape, 1)
        cell = ((in_pixel >> 6) == (out_pixel >> 4)) & (((in_pixel & 31) >> 1) == (out_pixel & 15))
        R.pool2[...] = jnp.where(cell, 0.25, 0.0).astype(FLOAT).astype(BFLOAT)

    def spread_matrices():
        back_shape = (px1, px2)
        in_pixel, out_pixel = iota(back_shape, 0), iota(back_shape, 1)
        cell = ((in_pixel >> 6) == (out_pixel >> 4)) & (((in_pixel & 31) >> 1) == (out_pixel & 15))
        R.spread2[...] = jnp.where(cell, 0.25, 0.0).astype(FLOAT).astype(BFLOAT)
        back_shape = (px1, px2 + two.W)
        in_pixel, out_pixel = iota(back_shape, 0), iota(back_shape, 1)
        down = (in_pixel >> 5) + 1 - 2 * (out_pixel >> 4)
        along = (in_pixel & 31) + 1 - 2 * (out_pixel & 15)
        R.spread3[...] = ones_where((down >= 0) & (down < 3) & (along >= 0) & (along < 3))

    pool_matrices()
    clear_rim(one, R.xh)
    if inside:
        gather_first.step()
    clear(R.a_sum)
    clear(R.keep1)
    clear(R.keep2)
    load_x.wait()
    halo_x.finish()
    if inside:
        gather_first.finish()
        unpack_rows(tag.r1)
        unpack_gains()
        gather_split.step()

    def prepare_rest():
        if inside:
            gather_small.step()
            pack_shards(tag.o1, tag.sh)
            gather_outer.step()
            pack_shards(tag.r2, tag.s2, tag.o2)
        build_masks(two)
        clear_rim(two, R.p1b)

    def window_split_sums():
        if inside:
            gather_outer.step()
        spread_matrices()
        clear_rim(one, R.dp2)
        clear_rim(two, R.dp2b)

        @pl.when(h == 0)
        def _():
            R.v1[:, :edge_rows, :] = jnp.zeros((NIM, edge_rows, C_MID), BFLOAT)

        @pl.when(h == nh - 1)
        def _():
            R.dq[:, px2:, :] = jnp.zeros((NIM, two.W, C_MID), BFLOAT)

    def window_gap():
        if inside:
            gather_small.finish()
            unpack_attention()
            gather_last.step()

    def window_mix():
        if inside:
            gather_outer.finish()
            unpack_rows(tag.sh)
            unpack_pairs(tag.o1)
            gather_last.step()

    def window_output():
        if inside:
            gather_last.step()
            gather_last.finish()
            unpack_rows(tag.r2)
            unpack_split(tag.s2)
            unpack_pairs(tag.o2)

    def first_sum(m, i, at):
        return (
            R.c_o1[m, 0:1, :] * R.o1[i, at, :]
            + R.c_sh[m, 0:1, :] * R.csh[i, at, :]
            + (R.c_o1[m, 1:2, :] + R.c_sh[m, 1:2, :])
        )

    one.halo, two.halo = {}, {}

    def chain(m):
        mine = images_of(m)

        def body(i):
            R.p1[i] = dot(R.xh[i], R.w_r1[...])

        over_images(m, body)
        exchange = Exchange(tag.n1, m)
        cells = jnp.zeros((8, LANES), FLOAT)
        for i in range(m * MB, (m + 1) * MB):
            cells = cells + fold(R.mk1[i, one.W : one.W + px1, :])
        exchange.start(
            stat_pass(m, R.p1, one.W, px1, C_MID, R.mk1, one.W)
            + [jnp.sum(cells, axis=0, keepdims=True)]
        )

        def body(i):
            R.t1[i] = dot(R.pool2[...], R.xh[i, edge_rows : edge_rows + px1, :]).astype(BFLOAT)

        over_images(m, body)
        when_last(m, prepare_rest)()
        total = yield from exchange.finish()
        R.counts[m : m + 1, :] = 1.0 / total[4:5, :]
        R.counts[2 + m : 3 + m, :] = 4.0 / total[4:5, :]
        norm_coef(m, R.c_n1, total, 0, C_MID, one, first.reduce)
        if inside and m == 0:
            gather_split.step()
        activate(m, one)
        if inside and m == 0:
            gather_split.finish()
            unpack_split(tag.s1)
        convolve(m, one)
        exchange = Exchange(tag.n2, m)
        exchange.start(stat_pass(m, R.p2, 0, px1, 2 * C_MID, R.mk1, one.W))
        when_last(m, window_split_sums)()
        total = yield from exchange.finish()
        norm_coef(m, R.c_n2, total, 0, 2 * C_MID, one, first.split)
        if inside and m == 0:
            gather_small.step()
        yield from attend(m, one, when_last(m, window_gap), nothing)
        mix(m, one, R.v1, edge_rows)
        halo = Halo((R.v1.at[mine, pl.ds(px1, edge_rows)], R.v1.at[mine, pl.ds(0, edge_rows)]))
        halo.start()
        when_last(m, window_mix)()
        yield
        product_out(m, R.t1, C_IN, R.w_sh, R.csh)
        exchange = Exchange(tag.no, m)
        exchange.put(stat_pass(m, R.csh, 0, px2, C_OUT, R.mk2, two.W), 16)
        halo.finish()

        def body(i):
            R.q1[i] = (dot(R.pool3[...], R.v1[i]) * (1.0 / 9.0)).astype(BFLOAT)

        over_images(m, body)
        product_out(m, R.q1, C_MID, R.w_o1, R.o1)
        exchange.put(stat_pass(m, R.o1, 0, px2, C_OUT, R.mk2, two.W), fill=False)
        exchange.send(0)
        when_last(m, window_output)()
        total = yield from exchange.finish()
        norm_coef(m, R.c_o1, total, 0, C_OUT, two, first.output)
        norm_coef(m, R.c_sh, total, 16, C_OUT, two, first.shortcut)

        def body(i):
            for t in range(0, px2, 16):
                at = slice(t, t + 16)
                value = first_sum(m, i, at)
                mask = widen(R.mk2[i, two.W + t : two.W + t + 16, :], C_OUT)
                R.l1[i, at, :] = (value * sigmoid(value) * mask).astype(BFLOAT)

        over_images(m, body)
        store_one = pltpu.make_async_copy(R.l1.at[mine], R.layer_one.at[mine], new_sem())
        store_one.start()
        late.append(store_one.wait)

        R.p1b[mine, two.W : two.W + px2, :] = dot(outer(m, R.l1, C_OUT), R.w_r2[...]).reshape(
            MB, px2, C_MID
        )
        exchange = Exchange(tag.n1b, m)
        exchange.start(
            stat_pass(m, R.p1b, two.W, px2, C_MID, R.mk2, two.W)
            + [jnp.sum(R.a_sum[m], axis=0, keepdims=True)]
        )
        halo = rims(m, two, R.p1b)
        halo.start()
        total = yield from exchange.finish()
        R.centre[m : m + 1, :] = take(total, 4, C_MID) * widen(R.counts[m : m + 1, :], C_MID)
        norm_coef(m, R.c_n1b, total, 0, C_MID, two, second.reduce)
        halo.finish()
        activate(m, two)
        convolve(m, two)
        exchange = Exchange(tag.n2b, m)
        exchange.start(stat_pass(m, R.p2b, 0, px2, 2 * C_MID, R.mk2, two.W))
        total = yield from exchange.finish()
        norm_coef(m, R.c_n2b, total, 0, 2 * C_MID, two, second.split)
        yield from attend(m, two, nothing, nothing)
        mix(m, two, R.mix2, 0)
        product_out(m, R.mix2, C_MID, R.w_o2, R.o2)
        exchange = Exchange(tag.nob, m)
        exchange.start(stat_pass(m, R.o2, 0, px2, C_OUT, R.mk2, two.W))
        if m == 0:
            load_cot.wait()
        total = yield from exchange.finish()
        norm_coef(m, R.c_o2, total, 0, C_OUT, two, second.output)

        clear_acc(m, 2, C_OUT)

        def body(i):
            total, along = R.acc[m, 0], R.acc[m, 1]
            for t in range(0, px2, 16):
                at = slice(t, t + 16)
                mask = widen(R.mk2[i, two.W + t : two.W + t + 16, :], C_OUT)
                raw = R.o2[i, at, :]
                value = R.c_o2[m, 0:1, :] * raw + R.c_o2[m, 1:2, :] + R.l1[i, at, :].astype(FLOAT)
                logistic = sigmoid(value)
                R.dpo[i, at, :] = (value * logistic * mask).astype(BFLOAT)
                grad = (
                    R.cot[i, at, :].astype(FLOAT) * mask * (logistic * (1.0 + value * (1.0 - logistic)))
                )
                R.g2[i, at, :] = grad
                total = total + fold(grad)
                along = along + fold(grad * (R.c_o2[m, 2:3, :] * raw + R.c_o2[m, 3:4, :]))
            R.acc[m, 0] = total
            R.acc[m, 1] = along

        over_images(m, body)
        exchange = Exchange(tag.dnob, m)
        exchange.start(totals(m, 2, C_OUT))
        store_two = pltpu.make_async_copy(R.dpo.at[mine], R.layer_two.at[mine], new_sem())
        store_two.start()
        total = yield from exchange.finish()
        norm_coef_back(m, R.c_o2, total, 0, 8, C_OUT, two, second.output)
        store_two.wait()
        norm_back(m, px2, R.g2, R.c_o2, R.o2, 0, R.mk2, two.W, R.dpo, 0, C_OUT)
        R.dmixb[mine] = dot(outer(m, R.dpo, C_OUT), R.w_o2[...], NT).reshape(MB, px2, C_MID)
        yield from splat_back(
            m,
            two,
            when_last(
                m, gradients_sent, grad_outer(tag.o2, R.mix2, C_MID, R.dpo), step_of(tag.o2)
            ),
            when_last(m, lambda: small_grads(two, False), step_of(tag.o2)),
            when_last(
                m,
                lambda: small_grads(two, True),
                step_of(tag.o2),
                small_two.start if inside else nothing,
            ),
            when_last(m, grad_split(two), step_of(tag.s2), step_of(tag.o2)),
            when_last(m, step_of(tag.s2)),
        )

        clear_acc(m, 3, C_OUT)
        R.o2[mine] = dot(outer(m, R.dp1b, C_MID), R.w_r2[...], NT).reshape(MB, px2, C_OUT)

        def body(i):
            sums_ = [R.acc[m, kind] for kind in range(3)]
            for t in range(0, px2, 16):
                at = slice(t, t + 16)
                mask = widen(R.mk2[i, two.W + t : two.W + t + 16, :], C_OUT)
                value = first_sum(m, i, at)
                grad = (R.g2[i, at, :] + R.o2[i, at, :]) * mask * slope_of(value)
                R.g2[i, at, :] = grad
                sums_[0] = sums_[0] + fold(grad)
                sums_[1] = sums_[1] + fold(
                    grad * (R.c_o1[m, 2:3, :] * R.o1[i, at, :] + R.c_o1[m, 3:4, :])
                )
                sums_[2] = sums_[2] + fold(
                    grad * (R.c_sh[m, 2:3, :] * R.csh[i, at, :] + R.c_sh[m, 3:4, :])
                )
            for kind in range(3):
                R.acc[m, kind] = sums_[kind]

        over_images(m, body)
        exchange = Exchange(tag.dno, m)
        exchange.start(totals(m, 3, C_OUT))
        when_last(m, grad_reduce_two, step_of(tag.r2), step_of(tag.s2))()
        total = yield from exchange.finish()
        norm_coef_back(m, R.c_o1, total, 0, 8, C_OUT, two, first.output)
        norm_coef_back(m, R.c_sh, total, 0, 16, C_OUT, two, first.shortcut)
        norm_back(m, px2, R.g2, R.c_o1, R.o1, 0, R.mk2, two.W, R.dpo, 0, C_OUT)
        R.dq[mine, :px2, :] = (
            (dot(outer(m, R.dpo, C_OUT), R.w_o1[...], NT) * (1.0 / 9.0))
            .astype(BFLOAT)
            .reshape(MB, px2, C_MID)
        )
        halo = Halo(up=(R.dq.at[mine, pl.ds(0, two.W)], R.dq.at[mine, pl.ds(px2, two.W)]))
        halo.start()
        norm_back(m, px2, R.g2, R.c_sh, R.csh, 0, R.mk2, two.W, R.cot, 0, C_OUT)
        when_last(m, step_of(tag.r2), step_of(tag.s2))()
        yield
        halo.finish()

        def body(i):
            R.dmix[i] = dot(R.spread3[...], R.dq[i])

        over_images(m, body)

        def window_split():
            R.t1[...] = (
                dot(R.cot[...].reshape(NIM * px2, C_OUT), R.w_sh[...], NT)
                .astype(BFLOAT)
                .reshape(NIM, px2, C_IN)
            )
            small_grads(one, True)
            if inside:
                emit_squeezes()
                small_one.start()

        def finish_two():
            if inside:
                R.d_e2[...] = small_two.finish()

        yield from splat_back(
            m,
            one,
            when_last(
                m,
                grad_outer(tag.o1, R.q1, C_MID, R.dpo),
                grad_outer(tag.sh, R.t1, C_IN, R.cot),
                step_of(tag.mid),
                step_of(tag.r2),
            ),
            when_last(m, lambda: small_grads(one, False), step_of(tag.mid), hand_out(tag.o2, tag.s2)),
            when_last(m, window_split, step_of(tag.mid), step_of(tag.r2)),
            when_last(m, grad_split(one), step_of(tag.s1)),
            when_last(m, step_of(tag.s1), step_of(tag.mid), hand_out(tag.r2, tag.o1, tag.sh), finish_two),
        )
        term = dot(rows_of(R.xh, m * MB, MB, edge_rows, px1, slice(0, C_IN)), rows_of(R.dp1, m * MB, MB, 0, px1, slice(0, C_MID)), TN)
        if m == 0:
            R.grad[:C_IN, :] = term
        else:
            emit(tag.r1, 0, R.grad[:C_IN, :] + term)

    chains = [chain(m) for m in range(MICRO)]
    while chains:
        for one_chain in list(chains):
            if next(one_chain, tag) is tag:
                chains.remove(one_chain)

    if inside:
        sums[tag.r1].step()
        sums[tag.s1].step()
    store_images = new_sem()
    own = pl.ds(edge_rows, px1)

    def image_grads(m):
        one.halo[m].sent()

        def body(i):
            value = dot(R.dp1[i], R.w_r1[...], NT) + dot(R.spread2[...], R.t1[i])
            R.dp2[i, own, :] = value.astype(BFLOAT)
            pltpu.make_async_copy(R.dp2.at[i, own], R.grad_images.at[i], store_images).start()

        over_images(m, body)

    image_grads(0)
    if inside:
        sums[tag.r1].step()
    image_grads(1)
    if inside:
        sums[tag.r1].step()
        sums[tag.s1].step()
        deliver(tag.s1)
        R.d_s1[...] = R.d_s1[...] + mean_term()
        total = small_one.finish()
        R.d_q1[...] = total[:8]
        R.d_q2[...] = total[8:16]
        R.d_e1[...] = total[16:]
    index = d * nh + h
    for full, target, length in (
        (R.all_gains, R.d_gains, GAIN_LEN // (nd * nh)),
        (R.all_shifts, R.d_shifts, SHIFT_LEN // (nd * nh)),
    ):
        start = index * length
        lane = start & (LANES - 1)
        turned = pltpu.roll(full[pl.ds(start >> 7, 8), :], lax.rem(LANES - lane, LANES), 1)
        here = iota((2, LANES), 1) < LANES - lane
        target[...] = jnp.where(here, turned[0:2], turned[1:3])
    if inside:
        sums[tag.r1].step()
        deliver(tag.r1)
        for group in sums.values():
            assert group.phase == 3
    wait_for(R.dp2.at[:, own], store_images)
    for wait in late:
        wait()


def per_device(nd, nh, images, size_group, cotangent, *params):
    weights, (norm_gains, norm_shifts) = params[:11], params[11:]
    devices = nd * nh
    rows = images.shape[1]
    px1 = rows * H
    px2 = px1 // 4
    hp1, hp2 = px1 + 2 * H, px2 + H
    per_rows = {name: weight.shape[0] // LANES for name, weight in zip(SHAPES, weights)}
    inside = (
        nh == 4
        and devices == 32
        and per_rows[tag.q1] == 8
        and all(inner % devices == 0 for inner, _ in SHAPES.values())
    )
    axes = (tag.dp, tag.height)
    index = lax.axis_index(axes)
    cfg = types.SimpleNamespace(nd=nd, nh=nh, inside=inside, rows=rows)

    operands, names, specs = [], [], []
    whole = pl.BlockSpec(memory_space=pltpu.VMEM)

    def operand(name, value, spec=whole):
        operands.append(value)
        names.append(name)
        specs.append(spec)

    operand(tag.groups, size_group, pl.BlockSpec(memory_space=pltpu.SMEM))
    operand(tag.images, images.reshape(NIM, px1, C_IN), pl.BlockSpec(memory_space=pl.ANY))
    operand(tag.cotangent, cotangent.reshape(NIM, px2, C_OUT), pl.BlockSpec(memory_space=pl.ANY))
    if inside:
        pieces = []
        for vector in (norm_gains, norm_shifts):
            lane = lax.rem(index * vector.shape[0], LANES)
            piece = lax.dynamic_update_slice(jnp.zeros((3 * LANES,), BFLOAT), vector, (lane,))
            pieces.append(piece.reshape(3, LANES))
        operand(tag.gs, jnp.pad(jnp.concatenate(pieces, axis=0), ((0, 10), (0, 0))))
        for name, weight in zip(SHAPES, weights):
            operand(tag.a_ + name, weight.reshape(-1, LANES))
        cfg.table, total_rows = row_table(per_rows)
        summed_rows = sum(cfg.table[tag.r1])
    else:
        for name, weight in zip(SHAPES, weights):
            full = lax.all_gather(weight, axes, axis=0, tiled=True).reshape(SHAPES[name])
            operand(tag.w_ + name, full.astype(FLOAT) if name[0] in "qe" else full)
        for name, vector, length in (
            (tag.gains, norm_gains, GAIN_ROWS),
            (tag.shifts, norm_shifts, SHIFT_ROWS),
        ):
            full = lax.all_gather(vector, axes, axis=0, tiled=True).astype(FLOAT)
            full = jnp.pad(full, (0, length * LANES - full.shape[0]))
            operand(name, full.reshape(length, LANES))

    outs = dict(
        layer_one=((NIM, px2, C_OUT), BFLOAT),
        layer_two=((NIM, px2, C_OUT), BFLOAT),
        grad_images=((NIM, px1, C_IN), BFLOAT),
    )
    for name, shape in SHAPES.items():
        outs["d_" + name] = ((per_rows[name], LANES) if inside else shape, FLOAT)
    outs[tag.d_gains] = ((2, LANES), FLOAT)
    outs[tag.d_shifts] = ((2, LANES), FLOAT)

    scratch = dict(
        xh=((NIM, hp1, C_IN), BFLOAT),
        cot=((NIM, px2, C_OUT), BFLOAT),
        mk1=((NIM, hp1, LANES), FLOAT),
        mk2=((NIM, hp2, LANES), FLOAT),
        edge1=((2, hp1, LANES), FLOAT),
        edge2=((2, MB * px2, LANES), FLOAT),
        counts=((8, LANES), FLOAT),
        all_gains=((GAIN_ROWS, LANES), FLOAT),
        all_shifts=((SHIFT_ROWS, LANES), FLOAT),
        a_sum=((MICRO, 8, C_MID), FLOAT),
        centre=((8, C_MID), FLOAT),
        grad_sum=((8, 2 * C_MID), FLOAT),
        acc=((MICRO, 3, 8, C_OUT), FLOAT),
        image_sums=((NIM, 8, 2 * C_MID), FLOAT),
        p1=((NIM, hp1, C_MID), FLOAT),
        a3=((NIM, hp1, 3 * C_MID), BFLOAT),
        p2=((NIM, px1, 2 * C_MID), FLOAT),
        s=((NIM, px1, 2 * C_MID), FLOAT),
        v1=((NIM, px1 + H, C_MID), BFLOAT),
        q1=((NIM, px2, C_MID), BFLOAT),
        t1=((NIM, px2, C_IN), BFLOAT),
        o1=((NIM, px2, C_OUT), FLOAT),
        csh=((NIM, px2, C_OUT), FLOAT),
        p1b=((NIM, hp2, C_MID), FLOAT),
        a3b=((NIM, hp2, 3 * C_MID), BFLOAT),
        p2b=((NIM, px2, 2 * C_MID), FLOAT),
        sb=((NIM, px2, 2 * C_MID), FLOAT),
        mix2=((NIM, px2, C_MID), BFLOAT),
        l1=((NIM, px2, C_OUT), BFLOAT),
        o2=((NIM, px2, C_OUT), FLOAT),
        g2=((NIM, px2, C_OUT), FLOAT),
        dpo=((NIM, px2, C_OUT), BFLOAT),
        dmixb=((NIM, px2, C_MID), FLOAT),
        dp2b=((NIM, hp2, 2 * C_MID), BFLOAT),
        dp1b=((NIM, px2, C_MID), BFLOAT),
        dq=((NIM, px2 + H // 2, C_MID), BFLOAT),
        dmix=((NIM, px1, C_MID), FLOAT),
        dp2=((NIM, hp1, 2 * C_MID), BFLOAT),
        dp1=((NIM, px1, C_MID), BFLOAT),
        grad=((9 * C_MID // 2, C_MID), FLOAT),
        pool3=((px2, px1 + H), BFLOAT),
        pool2=((px2, px1), BFLOAT),
        spread2=((px1, px2), BFLOAT),
        spread3=((px1, px2 + H // 2), BFLOAT),
        keep1=((MICRO, 8, 8, 2 * C_MID), FLOAT),
        keep2=((MICRO, 8, 8, 2 * C_MID), FLOAT),
        att1=((NIM, 8, 2 * C_MID), FLOAT),
        att2=((NIM, 8, 2 * C_MID), FLOAT),
        dgap1=((NIM, 8, C_MID), FLOAT),
        dgap2=((NIM, 8, C_MID), FLOAT),
        c_n1=((MICRO, 8, C_MID), FLOAT),
        c_n2=((MICRO, 8, 2 * C_MID), FLOAT),
        c_o1=((MICRO, 8, C_OUT), FLOAT),
        c_sh=((MICRO, 8, C_OUT), FLOAT),
        c_n1b=((MICRO, 8, C_MID), FLOAT),
        c_n2b=((MICRO, 8, 2 * C_MID), FLOAT),
        c_o2=((MICRO, 8, C_OUT), FLOAT),
    )
    for name, (count, lanes, kind) in SYNCS.items():
        for k, size in enumerate(stage_sizes(kind, nd, nh)):
            for m in range(MICRO):
                scratch["sy_" + name + str(m) + str(k)] = ((size, count, lanes), FLOAT)
    if inside:
        four = (nd // 2, 2, nh // 2, 2)
        scratch |= dict(
            pack=(four + (total_rows, LANES), BFLOAT),
            rc=(four[:3] + (summed_rows, LANES), BFLOAT),
            rp=((3,) + four[:1] + (summed_rows, LANES), BFLOAT),
            rz=((four[0] - 1, summed_rows, LANES), BFLOAT),
            small=((nd, nh, 48, LANES), FLOAT),
            small_in=((nd, 48, LANES), FLOAT),
            gains=((GAIN_ROWS, LANES), FLOAT),
            shifts=((SHIFT_ROWS, LANES), FLOAT),
            g_q1=((C_MID, C_ATT), FLOAT),
            g_q2=((C_MID, C_ATT), FLOAT),
        )
        for name, shape in SHAPES.items():
            scratch["w_" + name] = (shape, FLOAT if name[0] in "qe" else BFLOAT)

    results = pl.pallas_call(
        functools.partial(
            kernel, cfg, names + list(outs) + list(scratch) + [tag.sem]
        ),
        out_shape=[jax.ShapeDtypeStruct(shape, kind) for shape, kind in outs.values()],
        in_specs=specs,
        out_specs=[pl.BlockSpec(memory_space=pl.ANY)] * 3 + [whole] * (len(outs) - 3),
        scratch_shapes=[pltpu.VMEM(shape, kind) for shape, kind in scratch.values()]
        + [pltpu.SemaphoreType.DMA((SEMAPHORES,))],
        compiler_params=pltpu.CompilerParams(
            collective_id=0, has_side_effects=True, vmem_limit_bytes=62 * 1024 * 1024
        ),
    )(*operands)

    if inside:
        results = deliver_all(results)
    layer_one, layer_two, grad_images = results[:3]
    grads = [grad.reshape(-1) for grad in results[3:14]]
    if not inside:
        grads = [
            lax.psum_scatter(grad, axes, scatter_dimension=0, tiled=True) for grad in grads
        ]
    tails = [
        total.reshape(-1)[: vector.shape[0]] for total, vector in zip(results[14:], (norm_gains, norm_shifts))
    ]
    return (
        layer_one.reshape(cotangent.shape),
        layer_two.reshape(cotangent.shape),
        grad_images.reshape(images.shape),
        *grads,
        *tails,
    )


def copy_all(count, *refs):
    copies = [
        pltpu.make_async_copy(source, target, refs[-1].at[k])
        for k, (source, target) in enumerate(zip(refs[:count], refs[count : 2 * count]))
    ]
    for copy in copies:
        copy.start()
    for copy in copies:
        copy.wait()


def deliver_all(results):
    count = len(results)
    anywhere = pl.BlockSpec(memory_space=pl.ANY)
    return pl.pallas_call(
        functools.partial(copy_all, count),
        out_shape=[jax.ShapeDtypeStruct(value.shape, value.dtype) for value in results],
        in_specs=[pl.BlockSpec(memory_space=pltpu.VMEM)] * count,
        out_specs=[anywhere] * count,
        scratch_shapes=[pltpu.SemaphoreType.DMA((count,))],
    )(*results)


def solution(mesh):
    shard = P(("dp", "height"))
    rows = P("dp", "height", None, None)
    return jax.shard_map(
        functools.partial(per_device, mesh.shape["dp"], mesh.shape["height"]),
        mesh=mesh,
        in_specs=(rows, P("dp"), rows) + (shard,) * 13,
        out_specs=(rows,) * 3 + (shard,) * 13,
        check_vma=False,
    )
```

time: 236 us -> 217 us (0.919)
  Pallas kernels: 233 us -> 214 us
    pallas_call x1, Pallas kernels: 229 us -> 210 us  [per_device(): pl.pallas_call(functools.partial(kernel, cfg, names + list(outs) + list(s...]
where the time goes in v1:
time: 217 us
  Pallas kernels  214 us (99%)
    pallas_call x1, Pallas kernels, per_device(): pl.pallas_call(functools.partial(kernel, cfg, names + list(outs) + list(s...  210 us

profile of v1, /device:TPU:0, one launch (start us, length us, event | category | flops | bytes accessed | tf_op | source)
XLA Modules:
  0.0 216.8 jit_solution(14873138638702851806)
XLA Ops:
  0.7 0.9 dynamic_update_slice.7
  1.5 0.8 dynamic_update_slice.6
  2.4 0.6 fusion.2.refs_3_
  3.0 209.7 %shard_map.279 = (bf16[6,64,1024]{2,1,0:T(8,128)(2,1)}, bf16[6,64,1024]{2,1,0:T(8,128)(2,1)}, bf16[6,256,512]{2,1,0:T(8,128)(2,1)}, f32[32,128]{1,0:T(8,128)}, f...) custom-call(s32[6]{0:T(128)} %refs_0_.1, ...), custom_call_target="tpu_custom_call" | custom-call | tf_op jit(solution)/shard_map/pallas_call | solution.py:1698
  212.7 3.9 %shard_map.280 = (bf16[6,64,1024]{2,1,0:T(8,128)(2,1)}, bf16[6,64,1024]{2,1,0:T(8,128)(2,1)}, bf16[6,256,512]{2,1,0:T(8,128)(2,1)}, f32[32,128]{1,0:T(8,128)}, f...) custom-call(bf16[6,64,1024]{2,1,0:T(8,128)(2,1)} %get-tuple-element., ...), custom_call_target="tpu_custom_call" | custom-call | tf_op jit(solution)/shard_map/pallas_call | solution.py:1746
  (2 shorter events, 0.0 us)

commit v2 on v1

--- a/solution.py
+++ b/solution.py
@@ -73,7 +73,7 @@
     dn2=(8, LANES, ONCE),
     dn1=(8, LANES, ONCE),
 )
-SEMAPHORES = 384
+SEMAPHORES = 640
 SMALL = dict(e2=0, q=16, e1=32)
 
 
@@ -267,12 +267,14 @@
             self.put(vectors)
             self.send(0)
 
-        def finish(self):
+        def finish(self, between=None):
             for stage, (count, me, _) in enumerate(self.stages):
                 buf = self.bufs[stage]
                 if stage > 0:
                     buf[me] = total
                     self.send(stage)
+                    if between is not None and stage == 1:
+                        between()
                 yield
                 wait_for(buf.at[pl.ds(0, count - 1)], self.receive)
                 total = jnp.sum(buf[...], axis=0)
@@ -342,8 +344,9 @@
                     wait()
 
         class Scatter:
-            def __init__(self, start, stop):
+            def __init__(self, start, stop, direct=False):
                 self.rows = pl.ds(start, stop - start)
+                self.direct = direct
                 self.phase = -1
                 self.waits = []
 
@@ -373,6 +376,18 @@
                         return 0
 
                     lax.fori_loop(0, Z, add, 0)
+                    if self.direct:
+                        count = Z * X * Y
+                        for step in range(1, count):
+                            to = lax.rem(d * Y + y + step, count)
+                            dd, yy = lax.div(to, Y), lax.rem(to, Y)
+                            self.begin(
+                                G.at[lax.div(dd, X), lax.rem(dd, X), yy, c, rows],
+                                R.rd.at[step - 1],
+                                (dd, yy * 2 + c),
+                            )
+                        self.phase = 2
+                        return
                     for step in range(1, X * Y):
                         xx, yy = in_plane(step)
                         self.begin(
@@ -404,6 +419,10 @@
             start, count = table[name]
             rows = pl.ds(start, count)
             total = G[z, x, y, c, rows].astype(FLOAT)
+            if name == tag.r1:
+                for k in range(Z * X * Y - 1):
+                    total = total + R.rd[k].astype(FLOAT)
+                return total
             for k in range(Z - 1):
                 total = total + R.rz[k, rows].astype(FLOAT)
             return total
@@ -420,6 +439,18 @@
                 rows, blocks = per_dev(name), SHAPES[name][1] // LANES
                 order = ones_where(shuffle(rows * blocks, rows, blocks))
                 own_rows(name, dot(order, getattr(R, "a_" + name)[...]))
+
+        def pack_gains():
+            clear(R.piece)
+            lane_of = iota((1, LANES), 1)
+            for k, length in enumerate((GAIN_LEN // (nd * nh), SHIFT_LEN // (nd * nh))):
+                lane = lax.rem((d * nh + h) * length, LANES)
+                turned = pltpu.roll(R.gs[...].astype(FLOAT), lane, 1)
+                upper, lower = turned[2 * k : 2 * k + 1], turned[2 * k + 1 : 2 * k + 2]
+                R.piece[3 * k : 3 * k + 1, :] = jnp.where(lane_of >= lane, upper, 0.0)
+                R.piece[3 * k + 1 : 3 * k + 2, :] = jnp.where(lane_of < lane, upper, lower)
+                R.piece[3 * k + 2 : 3 * k + 3, :] = jnp.where(lane_of < lane, lower, 0.0)
+            own_rows(tag.gs, R.piece[...])
 
         def pack_small():
             own_rows(
@@ -583,18 +614,28 @@
             return (table[parts[0]][0], table[parts[-1]][0] + table[parts[-1]][1])
 
         gather_first = Gather(*range_of(tag.r1, tag.gs), direct=True)
-        gather_split = Gather(*range_of(tag.s1))
-        gather_small = Gather(*range_of(tag.q, tag.e2), direct=True)
-        gather_outer = Gather(*range_of(tag.o1, tag.sh))
-        gather_last = Gather(*range_of(tag.r2, tag.o2))
-        sums = dict(
-            o2=Scatter(*range_of(tag.o2)),
-            s2=Scatter(*range_of(tag.s2)),
-            r2=Scatter(*range_of(tag.r2)),
-            mid=Scatter(*range_of(tag.o1, tag.sh)),
-            s1=Scatter(*range_of(tag.s1)),
-            r1=Scatter(*range_of(tag.r1)),
-        )
+        def pieces(kind):
+            def halves(name):
+                start, stop = range_of(name)
+                middle = start + -(-(stop - start) // 32) * 16
+                return kind(start, middle), kind(middle, stop)
+
+            parts = types.SimpleNamespace(
+                s1=kind(*range_of(tag.s1)),
+                o1=kind(*range_of(tag.o1)),
+                r1=kind(*range_of(tag.r1)),
+                r2=kind(*range_of(tag.r2)),
+                o2=kind(*range_of(tag.o2)),
+            )
+            parts.sha, parts.shb = halves(tag.sh)
+            parts.s2a, parts.s2b = halves(tag.s2)
+            parts.s1a, parts.s1b = halves(tag.s1)
+            return parts
+
+        got = pieces(Gather)
+        got.small = Gather(*range_of(tag.q, tag.e2))
+        sums = pieces(Scatter)
+        sums.r1 = Scatter(*range_of(tag.r1), direct=True)
         small_two, small_one = SmallScatter(0, 16), SmallScatter(16, 32)
     else:
 
@@ -1097,8 +1138,33 @@
 
         return window
 
-    def step_of(name):
-        return sums[name].step if inside else nothing
+    def step_of(*parts):
+        def step():
+            if inside:
+                for name in parts:
+                    getattr(sums, name).step()
+
+        return step
+
+    def fetch(*parts):
+        def step():
+            if inside:
+                for name in parts:
+                    getattr(got, name).step()
+
+        return step
+
+    def run(*steps):
+        for step in steps:
+            step()
+
+    def unpack(how, *parts):
+        def step():
+            if inside:
+                for name in parts:
+                    how(name)
+
+        return step
 
     def hand_out(*parts):
         def step():
@@ -1142,7 +1208,8 @@
 
     def gradients_sent():
         if inside:
-            for gather in (gather_first, gather_split, gather_small, gather_outer, gather_last):
+            gather_first.sent()
+            for gather in vars(got).values():
                 gather.sent()
 
     halo_x = Halo(
@@ -1163,15 +1230,16 @@
     load_cot.start()
     if inside:
         pack_shards(tag.r1)
-        own_rows(tag.gs, R.gs[...])
+        pack_gains()
     pl.semaphore_wait(barrier, partners)
     if inside:
         gather_first.step()
     halo_x.start()
     if inside:
         pack_shards(tag.s1)
-        gather_split.step()
+        got.s1.step()
         pack_small()
+        got.small.step()
     build_masks(one)
 
     def pool_matrices():
@@ -1209,20 +1277,19 @@
         gather_first.finish()
         unpack_rows(tag.r1)
         unpack_gains()
-        gather_split.step()
-
-    def prepare_rest():
+
+    def window_start():
         if inside:
-            gather_small.step()
+            got.s1.step()
+            got.small.step()
             pack_shards(tag.o1, tag.sh)
-            gather_outer.step()
+            got.o1.step()
             pack_shards(tag.r2, tag.s2, tag.o2)
         build_masks(two)
         clear_rim(two, R.p1b)
 
     def window_split_sums():
-        if inside:
-            gather_outer.step()
+        fetch(tag.o1, tag.small, tag.sha)()
         spread_matrices()
         clear_rim(one, R.dp2)
         clear_rim(two, R.dp2b)
@@ -1236,25 +1303,23 @@
             R.dq[:, px2:, :] = jnp.zeros((NIM, two.W, C_MID), BFLOAT)
 
     def window_gap():
+        fetch(tag.sha, tag.shb, tag.o1)()
         if inside:
-            gather_small.finish()
+            got.small.finish()
             unpack_attention()
-            gather_last.step()
 
     def window_mix():
+        fetch(tag.shb, tag.r2, tag.s2a, tag.o1, tag.sha)()
         if inside:
-            gather_outer.finish()
+            unpack_pairs(tag.o1)
+        fetch(tag.shb)()
+        if inside:
             unpack_rows(tag.sh)
-            unpack_pairs(tag.o1)
-            gather_last.step()
-
-    def window_output():
+
+    def window_second_conv():
+        fetch(tag.s2b, tag.o2, tag.s2a, tag.s2b)()
         if inside:
-            gather_last.step()
-            gather_last.finish()
-            unpack_rows(tag.r2)
             unpack_split(tag.s2)
-            unpack_pairs(tag.o2)
 
     def first_sum(m, i, at):
         return (
@@ -1285,16 +1350,16 @@
             R.t1[i] = dot(R.pool2[...], R.xh[i, edge_rows : edge_rows + px1, :]).astype(BFLOAT)
 
         over_images(m, body)
-        when_last(m, prepare_rest)()
+        when_last(m, window_start)()
         total = yield from exchange.finish()
         R.counts[m : m + 1, :] = 1.0 / total[4:5, :]
         R.counts[2 + m : 3 + m, :] = 4.0 / total[4:5, :]
         norm_coef(m, R.c_n1, total, 0, C_MID, one, first.reduce)
         if inside and m == 0:
-            gather_split.step()
+            got.s1.step()
         activate(m, one)
         if inside and m == 0:
-            gather_split.finish()
+            got.s1.finish()
             unpack_split(tag.s1)
         convolve(m, one)
         exchange = Exchange(tag.n2, m)
@@ -1302,9 +1367,9 @@
         when_last(m, window_split_sums)()
         total = yield from exchange.finish()
         norm_coef(m, R.c_n2, total, 0, 2 * C_MID, one, first.split)
-        if inside and m == 0:
-            gather_small.step()
-        yield from attend(m, one, when_last(m, window_gap), nothing)
+        yield from attend(
+            m, one, when_last(m, window_gap), when_last(m, fetch(tag.shb, tag.r2, tag.sha))
+        )
         mix(m, one, R.v1, edge_rows)
         halo = Halo((R.v1.at[mine, pl.ds(px1, edge_rows)], R.v1.at[mine, pl.ds(0, edge_rows)]))
         halo.start()
@@ -1322,8 +1387,12 @@
         product_out(m, R.q1, C_MID, R.w_o1, R.o1)
         exchange.put(stat_pass(m, R.o1, 0, px2, C_OUT, R.mk2, two.W), fill=False)
         exchange.send(0)
-        when_last(m, window_output)()
-        total = yield from exchange.finish()
+        when_last(m, fetch(tag.r2, tag.s2a, tag.s2b))()
+        total = yield from exchange.finish(
+            when_last(
+                m, fetch(tag.s2a, tag.s2b, tag.o2, tag.r2), unpack(unpack_rows, tag.r2) if inside else nothing
+            )
+        )
         norm_coef(m, R.c_o1, total, 0, C_OUT, two, first.output)
         norm_coef(m, R.c_sh, total, 16, C_OUT, two, first.shortcut)
 
@@ -1349,6 +1418,7 @@
         )
         halo = rims(m, two, R.p1b)
         halo.start()
+        when_last(m, window_second_conv)()
         total = yield from exchange.finish()
         R.centre[m : m + 1, :] = take(total, 4, C_MID) * widen(R.counts[m : m + 1, :], C_MID)
         norm_coef(m, R.c_n1b, total, 0, C_MID, two, second.reduce)
@@ -1357,9 +1427,15 @@
         convolve(m, two)
         exchange = Exchange(tag.n2b, m)
         exchange.start(stat_pass(m, R.p2b, 0, px2, 2 * C_MID, R.mk2, two.W))
+        when_last(m, fetch(tag.o2))()
         total = yield from exchange.finish()
         norm_coef(m, R.c_n2b, total, 0, 2 * C_MID, two, second.split)
-        yield from attend(m, two, nothing, nothing)
+        yield from attend(
+            m,
+            two,
+            when_last(m, fetch(tag.o2), unpack(unpack_pairs, tag.o2) if inside else nothing),
+            nothing,
+        )
         mix(m, two, R.mix2, 0)
         product_out(m, R.mix2, C_MID, R.w_o2, R.o2)
         exchange = Exchange(tag.nob, m)
@@ -1405,15 +1481,15 @@
             when_last(
                 m, gradients_sent, grad_outer(tag.o2, R.mix2, C_MID, R.dpo), step_of(tag.o2)
             ),
-            when_last(m, lambda: small_grads(two, False), step_of(tag.o2)),
+            when_last(m, step_of(tag.o2), lambda: small_grads(two, False)),
             when_last(
                 m,
-                lambda: small_grads(two, True),
                 step_of(tag.o2),
                 small_two.start if inside else nothing,
+                lambda: small_grads(two, True),
             ),
-            when_last(m, grad_split(two), step_of(tag.s2), step_of(tag.o2)),
-            when_last(m, step_of(tag.s2)),
+            when_last(m, grad_split(two), step_of(tag.s2a, tag.s2b, tag.o2)),
+            when_last(m, step_of(tag.s2a), hand_out(tag.o2)),
         )
 
         clear_acc(m, 3, C_OUT)
@@ -1440,8 +1516,8 @@
         over_images(m, body)
         exchange = Exchange(tag.dno, m)
         exchange.start(totals(m, 3, C_OUT))
-        when_last(m, grad_reduce_two, step_of(tag.r2), step_of(tag.s2))()
-        total = yield from exchange.finish()
+        when_last(m, step_of(tag.s2b, tag.s2a), grad_reduce_two, step_of(tag.r2))()
+        total = yield from exchange.finish(when_last(m, step_of(tag.r2, tag.s2b)))
         norm_coef_back(m, R.c_o1, total, 0, 8, C_OUT, two, first.output)
         norm_coef_back(m, R.c_sh, total, 0, 16, C_OUT, two, first.shortcut)
         norm_back(m, px2, R.g2, R.c_o1, R.o1, 0, R.mk2, two.W, R.dpo, 0, C_OUT)
@@ -1453,7 +1529,7 @@
         halo = Halo(up=(R.dq.at[mine, pl.ds(0, two.W)], R.dq.at[mine, pl.ds(px2, two.W)]))
         halo.start()
         norm_back(m, px2, R.g2, R.c_sh, R.csh, 0, R.mk2, two.W, R.cot, 0, C_OUT)
-        when_last(m, step_of(tag.r2), step_of(tag.s2))()
+        when_last(m, step_of(tag.r2, tag.s2a))()
         yield
         halo.finish()
 
@@ -1483,17 +1559,23 @@
             when_last(
                 m,
                 grad_outer(tag.o1, R.q1, C_MID, R.dpo),
+                step_of(tag.o1, tag.s2b, tag.r2),
+                hand_out(tag.s2),
+            ),
+            when_last(
+                m,
+                step_of(tag.o1),
+                lambda: small_grads(one, False),
                 grad_outer(tag.sh, R.t1, C_IN, R.cot),
-                step_of(tag.mid),
-                step_of(tag.r2),
+                step_of(tag.sha, tag.shb),
             ),
-            when_last(m, lambda: small_grads(one, False), step_of(tag.mid), hand_out(tag.o2, tag.s2)),
-            when_last(m, window_split, step_of(tag.mid), step_of(tag.r2)),
-            when_last(m, grad_split(one), step_of(tag.s1)),
-            when_last(m, step_of(tag.s1), step_of(tag.mid), hand_out(tag.r2, tag.o1, tag.sh), finish_two),
+            when_last(m, step_of(tag.o1, tag.sha), window_split, hand_out(tag.r2)),
+            when_last(m, step_of(tag.shb), grad_split(one), step_of(tag.s1a, tag.s1b, tag.sha, tag.o1)),
+            when_last(m, step_of(tag.s1a, tag.shb, tag.sha), hand_out(tag.o1), finish_two),
         )
         term = dot(rows_of(R.xh, m * MB, MB, edge_rows, px1, slice(0, C_IN)), rows_of(R.dp1, m * MB, MB, 0, px1, slice(0, C_MID)), TN)
         if m == 0:
+            step_of(tag.s1b)()
             R.grad[:C_IN, :] = term
         else:
             emit(tag.r1, 0, R.grad[:C_IN, :] + term)
@@ -1504,9 +1586,7 @@
             if next(one_chain, tag) is tag:
                 chains.remove(one_chain)
 
-    if inside:
-        sums[tag.r1].step()
-        sums[tag.s1].step()
+    step_of(tag.r1, tag.s1a)()
     store_images = new_sem()
     own = pl.ds(edge_rows, px1)
 
@@ -1521,12 +1601,12 @@
         over_images(m, body)
 
     image_grads(0)
+    step_of(tag.r1, tag.s1b)()
+    image_grads(1)
+    step_of(tag.shb, tag.s1a)()
+    hand_out(tag.sh)()
     if inside:
-        sums[tag.r1].step()
-    image_grads(1)
-    if inside:
-        sums[tag.r1].step()
-        sums[tag.s1].step()
+        sums.s1b.step()
         deliver(tag.s1)
         R.d_s1[...] = R.d_s1[...] + mean_term()
         total = small_one.finish()
@@ -1544,10 +1624,10 @@
         here = iota((2, LANES), 1) < LANES - lane
         target[...] = jnp.where(here, turned[0:2], turned[1:3])
     if inside:
-        sums[tag.r1].step()
+        sums.r1.step()
         deliver(tag.r1)
-        for group in sums.values():
-            assert group.phase == 3
+        for name, group in list(vars(sums).items()) + list(vars(got).items()):
+            assert group.phase in (-1, 3), name
     wait_for(R.dp2.at[:, own], store_images)
     for wait in late:
         wait()
@@ -1583,16 +1663,15 @@
     operand(tag.images, images.reshape(NIM, px1, C_IN), pl.BlockSpec(memory_space=pl.ANY))
     operand(tag.cotangent, cotangent.reshape(NIM, px2, C_OUT), pl.BlockSpec(memory_space=pl.ANY))
     if inside:
-        pieces = []
-        for vector in (norm_gains, norm_shifts):
-            lane = lax.rem(index * vector.shape[0], LANES)
-            piece = lax.dynamic_update_slice(jnp.zeros((3 * LANES,), BFLOAT), vector, (lane,))
-            pieces.append(piece.reshape(3, LANES))
-        operand(tag.gs, jnp.pad(jnp.concatenate(pieces, axis=0), ((0, 10), (0, 0))))
+        pieces = [
+            jnp.pad(vector, (0, 2 * LANES - vector.shape[0])).reshape(2, LANES)
+            for vector in (norm_gains, norm_shifts)
+        ]
+        operand(tag.gs, jnp.pad(jnp.concatenate(pieces, axis=0), ((0, 12), (0, 0))))
         for name, weight in zip(SHAPES, weights):
             operand(tag.a_ + name, weight.reshape(-1, LANES))
         cfg.table, total_rows = row_table(per_rows)
-        summed_rows = sum(cfg.table[tag.r1])
+        summed_rows, phased_rows = sum(cfg.table[tag.r1]), cfg.table[tag.r1][0]
     else:
         for name, weight in zip(SHAPES, weights):
             full = lax.all_gather(weight, axes, axis=0, tiled=True).reshape(SHAPES[name])
@@ -1683,8 +1762,10 @@
         scratch |= dict(
             pack=(four + (total_rows, LANES), BFLOAT),
             rc=(four[:3] + (summed_rows, LANES), BFLOAT),
-            rp=((3,) + four[:1] + (summed_rows, LANES), BFLOAT),
-            rz=((four[0] - 1, summed_rows, LANES), BFLOAT),
+            rp=((3,) + four[:1] + (phased_rows, LANES), BFLOAT),
+            rz=((four[0] - 1, phased_rows, LANES), BFLOAT),
+            rd=((devices // 2 - 1, per_rows[tag.r1], LANES), BFLOAT),
+            piece=((16, LANES), FLOAT),
             small=((nd, nh, 48, LANES), FLOAT),
             small_in=((nd, 48, LANES), FLOAT),
             gains=((GAIN_ROWS, LANES), FLOAT),
@@ -1730,14 +1811,16 @@
 
 
 def copy_all(count, *refs):
-    copies = [
-        pltpu.make_async_copy(source, target, refs[-1].at[k])
-        for k, (source, target) in enumerate(zip(refs[:count], refs[count : 2 * count]))
-    ]
-    for copy in copies:
-        copy.start()
-    for copy in copies:
-        copy.wait()
+    sources, targets, held, sem = refs[:count], refs[count : 2 * count], refs[2 * count : -1], refs[-1]
+    loads = [pltpu.make_async_copy(sources[k], held[k], sem.at[0, k]) for k in range(count)]
+    stores = [pltpu.make_async_copy(held[k], targets[k], sem.at[1, k]) for k in range(count)]
+    for load in loads:
+        load.start()
+    for load, store in zip(loads, stores):
+        load.wait()
+        store.start()
+    for store in stores:
+        store.wait()
 
 
 def deliver_all(results):
@@ -1746,9 +1829,10 @@
     return pl.pallas_call(
         functools.partial(copy_all, count),
         out_shape=[jax.ShapeDtypeStruct(value.shape, value.dtype) for value in results],
-        in_specs=[pl.BlockSpec(memory_space=pltpu.VMEM)] * count,
+        in_specs=[anywhere] * count,
         out_specs=[anywhere] * count,
-        scratch_shapes=[pltpu.SemaphoreType.DMA((count,))],
+        scratch_shapes=[pltpu.VMEM(value.shape, value.dtype) for value in results]
+        + [pltpu.SemaphoreType.DMA((2, count))],
     )(*results)
 
 

time: 217 us -> 197 us (0.908)
  Pallas kernels: 214 us -> 194 us
    pallas_call x1, Pallas kernels: 210 us -> 191 us  [per_device(): pl.pallas_call(functools.partial(kernel, cfg, names + list(outs) + list(s...]
where the time goes in v2:
time: 197 us; the launch traced here: 196 us
  Pallas kernels  194 us (98%)
    pallas_call x1, Pallas kernels, per_device(): pl.pallas_call(functools.partial(kernel, cfg, names + list(outs) + list(s...  191 us

profile of v2, /device:TPU:0, one launch (start us, length us, event | category | flops | bytes accessed | tf_op | source)
XLA Modules:
  0.0 196.3 jit_solution(11090053762004390061)
XLA Ops:
  0.6 0.7 pad_bitcast_fusion
  1.3 0.6 fusion.2.refs_3_
  1.9 190.7 %shard_map.279 = (bf16[6,64,1024]{2,1,0:T(8,128)(2,1)}, bf16[6,64,1024]{2,1,0:T(8,128)(2,1)}, bf16[6,256,512]{2,1,0:T(8,128)(2,1)}, f32[32,128]{1,0:T(8,128)}, f...) custom-call(s32[6]{0:T(128)} %refs_0_.1, ...), custom_call_target="tpu_custom_call" | custom-call | tf_op jit(solution)/shard_map/pallas_call | solution.py:1779
  192.7 3.5 %shard_map.280 = (bf16[6,64,1024]{2,1,0:T(8,128)(2,1)}, bf16[6,64,1024]{2,1,0:T(8,128)(2,1)}, bf16[6,256,512]{2,1,0:T(8,128)(2,1)}, f32[32,128]{1,0:T(8,128)}, f...) custom-call(bf16[6,64,1024]{2,1,0:T(8,128)(2,1)} %get-tuple-element., ...), custom_call_target="tpu_custom_call" | custom-call | tf_op jit(solution)/shard_map/pallas_call | solution.py:1829
